TPU v7x, 32 devices: a whole 2x2x4 slice. The times are simulated.
32 devices in a mesh: grp: 2 (over y), seq: 4 (over z), ch: 2 (over x), sub: 2 (over core).
Axes of the slice: x: 2, y: 2, z: 4, core: 2. Of those that a mesh axis runs over, the one named last changes fastest.
Arguments:
- tokens: bfloat16 [8, 384, 4, 512], P('grp', ('ch', 'sub'), 'seq'), parts along dimension 0, may hold values from -6 to 6
- gate_scale: float32 [4, 384], P(None, ('ch', 'sub')), may hold values from -4 to 4
- gate_shift: float32 [4, 384], P(None, ('ch', 'sub')), may hold values from -4 to 4
- sequence_right_factor: bfloat16 [4, 512, 512], P('seq'), may hold values from -0.25 to 0.25
- sequence_left_factor: bfloat16 [512, 4, 4], P('seq'), may hold values from -3 to 3
- up_first: bfloat16 [2, 4, 1536, 384], P(None, None, ('ch', 'sub')), may hold values from -0.3125 to 0.3125
- up_second: bfloat16 [2, 1536, 4, 4], P(None, ('ch', 'sub')), may hold values from -3 to 3
- up_shift: float32 [2, 4, 1536], P(None, None, ('ch', 'sub')), may hold values from -3 to 3
- down_first: bfloat16 [384, 4, 1536], P(None, None, ('ch', 'sub')), may hold values from -0.15625 to 0.15625
- down_second: bfloat16 [384, 4, 4], P(('ch', 'sub')), may hold values from -3 to 3
- cotangent: bfloat16 [8, 384, 4, 512], P('grp', ('ch', 'sub'), 'seq'), parts along dimension 0, may hold values from -6 to 6
Outputs:
- layer_out: bfloat16 [8, 384, 4, 512], P('grp', ('ch', 'sub'), 'seq'), parts along dimension 0
- token_input_gradient: float32 [8, 384, 4, 512], P('grp', ('ch', 'sub'), 'seq'), parts along dimension 0
- right_factor_gradient: float32 [8, 512, 512], P(('grp', 'seq')), parts along dimension 0
- left_factor_gradient: float32 [1024, 4, 4], P(('grp', 'seq')), parts along dimension 0
- up_first_grad: float32 [4, 4, 1536, 384], P('grp', None, ('ch', 'sub')), parts along dimension 0
- down_first_grad: float32 [768, 4, 1536], P('grp', None, ('ch', 'sub')), parts along dimension 0
There are 2 independent parts, one for each index of `grp`. A program takes and returns all parts, laid end to end along the dimension named above; an argument that names none is the same for every part. Nothing has to cross between parts.
All inputs are finite; a program needn't handle non-finite values.
Results may differ from a plain program's by a relative error of at most 0.017.
Values may be sent and summed in bfloat16 or wider, within the bound.
A program may use at most 128 MiB of HBM per device.

v0:
```python
import jax
import jax.numpy as jnp
from jax import lax
from jax.sharding import PartitionSpec as P

top_precision = lax.Precision.HIGHEST


def gated_unit(stacked):
    return jax.nn.gelu(stacked[0]) * stacked[1]


def per_device(
    tokens,
    gate_scale,
    gate_shift,
    sequence_right_factor,
    sequence_left_factor,
    up_first,
    up_second,
    up_shift,
    down_first,
    down_second,
    cotangent,
):
    block_count, part_rows, seq_blocks, block_len = tokens.shape
    token_count = seq_blocks * block_len
    hidden_local = up_first.shape[2]
    section_local = jnp.einsum(
        "oaj,zuoj->zuoa", sequence_right_factor, tokens, preferred_element_type=jnp.float32
    ).astype(jnp.bfloat16)
    spread_tokens = lax.all_to_all(section_local, "seq", split_axis=3, concat_axis=2, tiled=True)
    mixed_spread = jnp.einsum(
        "hli,xoih->xolh", sequence_left_factor, spread_tokens, preferred_element_type=jnp.float32
    ).astype(jnp.bfloat16)
    sequence_mixed = lax.all_to_all(mixed_spread, "seq", split_axis=2, concat_axis=3, tiled=True)
    input_tokens = tokens.astype(jnp.float32)
    mixed_float = sequence_mixed.astype(jnp.float32)
    gating = jax.nn.sigmoid(
        input_tokens * gate_scale[:, :, None, None] + gate_shift[:, :, None, None]
    )
    seq_out = (input_tokens + gating * mixed_float).astype(jnp.bfloat16)
    flat_in = seq_out.reshape(block_count, part_rows, token_count)
    second_w = up_second.astype(jnp.float32)
    weights = up_first
    lifted = jnp.einsum(
        "gkqp,kpt->gkqt",
        weights,
        lax.all_gather(flat_in, ("ch", "sub"), axis=1, tiled=True),
        preferred_element_type=jnp.float32,
    )
    stacked = (
        jnp.einsum("gqjk,gkqt->gjqt", second_w, lifted, precision=top_precision)
        + up_shift[:, :, :, None]
    )
    hidden = gated_unit(stacked).astype(jnp.bfloat16)
    group_count = lax.axis_size(("ch", "sub"))
    all_down = lax.all_gather(down_first, ("ch", "sub"), axis=2, tiled=True)
    token_hidden = lax.all_to_all(hidden, ("ch", "sub"), split_axis=2, concat_axis=1, tiled=True)
    share_len = token_hidden.shape[2]
    grouped_h = token_hidden.reshape(block_count, group_count, hidden_local, share_len)
    grouped_v = all_down.reshape(all_down.shape[0], block_count, group_count, hidden_local)
    group_terms = jnp.einsum(
        "rjaq,jaqt->arjt", grouped_v, grouped_h, preferred_element_type=jnp.float32
    )
    share_sum = jnp.sum(group_terms.astype(jnp.bfloat16).astype(jnp.float32), axis=0)
    reduced = lax.all_to_all(
        share_sum.astype(jnp.bfloat16), ("ch", "sub"), split_axis=0, concat_axis=2, tiled=True
    ).astype(share_sum.dtype)
    output = jnp.einsum(
        "rkj,rjt->krt", down_second.astype(jnp.float32), reduced, precision=top_precision
    )
    layer_out = (flat_in.astype(jnp.float32) + output).astype(jnp.bfloat16).reshape(tokens.shape)
    upstream = cotangent.reshape(block_count, part_rows, token_count)
    down_cot = jnp.einsum(
        "rkj,krt->jrt", down_second, upstream, preferred_element_type=jnp.float32
    ).astype(jnp.bfloat16)
    portion = lax.all_gather(down_cot, ("ch", "sub"), axis=1, tiled=True)
    weights = down_first
    hidden_cot = jnp.einsum("rjq,jrt->jqt", weights, portion, preferred_element_type=jnp.float32)
    grad_rows = jnp.einsum("jrt,jqt->rjq", portion, hidden, preferred_element_type=jnp.float32)
    hidden_cot, down_grad = (hidden_cot, grad_rows)
    gate_pull = jax.vjp(gated_unit, stacked)[1]
    stacked_cot = gate_pull(hidden_cot)[0]
    lifted_cot = jnp.einsum(
        "gqjk,gjqt->gkqt", second_w, stacked_cot, precision=top_precision
    ).astype(jnp.bfloat16)
    grad_cols = jnp.einsum(
        "gkqt,kpt->gkqp",
        lifted_cot,
        lax.all_gather(flat_in, ("ch", "sub"), axis=1, tiled=True),
        preferred_element_type=jnp.float32,
    )
    first_grad = grad_cols
    first_grad, down_grad = (
        lax.psum(first_grad.astype(jnp.bfloat16), "seq").astype(jnp.float32),
        lax.psum(down_grad.astype(jnp.bfloat16), "seq").astype(jnp.float32),
    )
    weights = up_first
    input_cot = lax.psum_scatter(
        jnp.einsum(
            "gkqp,gkqt->pkt", weights, lifted_cot, preferred_element_type=jnp.float32
        ).astype(jnp.bfloat16),
        ("ch", "sub"),
        scatter_dimension=0,
        tiled=True,
    ).astype(jnp.float32)
    chan_cot = jnp.transpose(input_cot, (1, 0, 2)).reshape(tokens.shape)
    total_cot = cotangent.astype(jnp.float32) + chan_cot
    mixed_tangent = (total_cot * gating).astype(jnp.bfloat16)
    straight_path = (
        total_cot + total_cot * mixed_float * gating * (1.0 - gating) * gate_scale[:, :, None, None]
    )
    spread_tangent = lax.all_to_all(mixed_tangent, "seq", split_axis=3, concat_axis=2, tiled=True)
    section_spread = jnp.einsum(
        "vdy,medv->meyv", sequence_left_factor, spread_tangent, preferred_element_type=jnp.float32
    ).astype(jnp.bfloat16)
    left_factor_gradient = jnp.einsum(
        "zueo,zuho->oeh", spread_tangent, spread_tokens, preferred_element_type=jnp.float32
    )
    left_factor_gradient = lax.psum(
        left_factor_gradient.astype(jnp.bfloat16), ("ch", "sub")
    ).astype(jnp.float32)
    section_tangent = lax.all_to_all(section_spread, "seq", split_axis=2, concat_axis=3, tiled=True)
    right_factor_gradient = jnp.einsum(
        "advl,advu->vlu", section_tangent, tokens, preferred_element_type=jnp.float32
    )
    token_input_gradient = straight_path + jnp.einsum(
        "wmi,rfwm->rfwi", sequence_right_factor, section_tangent, preferred_element_type=jnp.float32
    )
    right_factor_gradient = lax.psum(
        right_factor_gradient.astype(jnp.bfloat16), ("ch", "sub")
    ).astype(jnp.float32)
    return (
        layer_out,
        token_input_gradient,
        right_factor_gradient,
        left_factor_gradient,
        first_grad,
        down_grad,
    )


def solution(mesh):
    placed = (
        P("grp", ("ch", "sub"), "seq", None),
        P(None, ("ch", "sub")),
        P(None, ("ch", "sub")),
        P("seq", None, None),
        P("seq", None, None),
        P(None, None, ("ch", "sub"), None),
        P(None, ("ch", "sub"), None, None),
        P(None, None, ("ch", "sub")),
        P(None, None, ("ch", "sub")),
        P(("ch", "sub"), None, None),
        P("grp", ("ch", "sub"), "seq", None),
    )
    return jax.shard_map(
        per_device,
        mesh=mesh,
        in_specs=placed,
        out_specs=(
            P("grp", ("ch", "sub"), "seq", None),
            P("grp", ("ch", "sub"), "seq", None),
            P(("grp", "seq"), None, None),
            P(("grp", "seq"), None, None),
            P("grp", None, ("ch", "sub"), None),
            P("grp", None, ("ch", "sub")),
        ),
        check_vma=False,
    )
```

profile of v0, /device:TPU:0, one launch (start us, length us, event | category | flops | bytes accessed | tf_op | source)
XLA Modules:
  0.0 403.6 jit_solution(17837902421233124451)
XLA Ops:
  10.0 6.3 %all-to-all-start = ((bf16[4,96,1,512]{1,0,2,3:T(4,128)(2,1)}), bf16[4,96,1,512]{1,0,2,3:T(4,128)(2,1)S(1)}, u32[]{:S(2)}, u32[]{:S(2)}) async-start(bf16[4,96,1,512]{1,0,2,3:T(4,128)(2,1)} %copy.244), calls=%async_computation | async-start | bytes 1048576 | tf_op jit(solution)/shard_map/all_to_all | solution.py:32
  16.5 14.3 %all-to-all-done = bf16[4,96,1,512]{1,0,2,3:T(4,128)(2,1)S(1)} async-done(((bf16[4,96,1,512]{1,0,2,3:T(4,128)(2,1)}), bf16[4,96,1,512]{1,0,2,3:T(4,128)(2,1)S(1)}, u32[]{:S(2)}, u32[]{:S(2)}) %all-to-all-start) | async-done | bytes 393248 | tf_op jit(solution)/shard_map/all_to_all | solution.py:32
  34.5 13.6 %all_to_all.75 = bf16[4,96,4,128]{3,1,0,2:T(8,128)(2,1)S(1)} all-to-all(bf16[4,96,4,128]{3,1,0,2:T(8,128)(2,1)S(1)} %copy.248), channel_id=1, replica_groups=mesh['grp'=2,'seq'=4,'ch'=2,'sub'=2] {'seq'}, dimensions={2} | all-to-all | bytes 786432 | tf_op jit(solution)/shard_map/all_to_all | solution.py:36
  52.4 2.2 fusion.53
  56.1 3.4 copy.260
  59.5 11.5 %all-gather.9.cloned.1.call-done = bf16[4,384,1,512]{3,0,2,1:T(4,128)(2,1)} async-done(((bf16[4,96,1,512]{3,0,2,1:T(4,128)(2,1)}), bf16[4,384,1,512]{3,0,2,1:T(4,128)(2,1)}) %all-gather.9.cloned.1.call-update) | async-done | bytes 1572880 | tf_op jit(solution)/shard_map/all_gather | solution.py:49
  71.1 3.9 copy.252
  74.9 5.9 %convolution_bitcast_fusion = f32[2,4,384,512]{2,3,0,1:T(8,128)} fusion(bf16[2,4,384,384]{3,2,1,0:T(8,128)(2,1)S(1)} %copy-done, bf16[4,384,1,512]{1,3,0,2:T(8,128)(2,1)} %copy.252), kind=kOutput, calls=%fused_computation.28 | convolution fusion | flops 1207959552 | bytes 10223616 | tf_op jit(solution)/shard_map/gkqp,kpt->gkqt/dot_general | solution.py:46
  80.8 8.0 %copy.254 = f32[2,4,384,512]{3,1,2,0:T(4,128)} copy(f32[2,4,384,512]{2,3,0,1:T(8,128)} %convolution_bitcast_fusion) | data formatting | bytes 12582912 | tf_op jit(solution)/shard_map/gkqp,kpt->gkqt/transpose | solution.py:46
  88.8 9.2 %fusion.83 = f32[2,384,512,4]{2,3,1,0:T(4,128)S(1)} fusion(f32[2,4,384,512]{3,1,2,0:T(4,128)} %copy.254, bf16[2,384,4,4]{2,3,1,0:T(4,128)(2,1)S(1)} %copy.273), kind=kOutput, calls=%fused_computation.93 | convolution fusion | flops 75497472 | bytes 12607488 | tf_op jit(solution)/shard_map/gqjk,gkqt->gjqt/dot_general | solution.py:53
  98.0 3.8 bitcast_add_fusion
  101.8 8.0 %fusion.11 = (f32[1,4,384,512]{3,2,1,0:T(8,128)S(1)}, f32[1,4,384,512]{3,2,1,0:T(8,128)S(1)}, bf16[4,384,512]{2,1,0:T(8,128)(2,1)}) fusion(f32[2,4,384,512]{3,2,1,0:T(8,128)} %bitcast_add_fusion, bf16[384,4,384]{0,2,1:T(8,128)(2,1)} %copy.260, bf16[4,384,512]{2,0,1:T(4,128)(2,1)} %all-gather.7.cloned.1.call-done), kind=kOutput, calls=%fused_computation.20 | convolution fusion | flops 622854144 | bytes 16908288 | tf_op jit(solution)/shard_map/rjq,jrt->jqt/dot_general | solution.py:80
  110.5 8.8 %convert_bitcast_fusion = bf16[2,4,384,512]{3,1,2,0:T(4,128)(2,1)S(1)} fusion(bf16[2,384,4,4]{2,3,1,0:T(4,128)(2,1)S(1)} %copy.273, f32[2,4,384,512]{3,2,1,0:T(8,128)S(1)} %pad_add_fusion), kind=kOutput, calls=%fused_computation.21 | convolution fusion | flops 77070336 | bytes 9461760 | tf_op jit(solution)/shard_map/gqjk,gjqt->gkqt/dot_general | solution.py:85
  121.0 3.0 fusion.34
  124.0 4.0 copy.276
  129.9 41.3 %all-reduce.10.cloned.1.call-done = bf16[384,4,512]{2,1,0:T(4,128)(2,1)} async-done(((bf16[384,4,512]{2,1,0:T(4,128)(2,1)}), bf16[384,4,512]{2,1,0:T(4,128)(2,1)}) %all-reduce.10.cloned.1.call-update) | async-done | bytes 1572880
  173.7 18.9 %all_to_all.76 = bf16[4,96,1,512]{1,0,2,3:T(4,128)(2,1)S(1)} all-to-all(bf16[4,96,1,512]{1,0,2,3:T(4,128)(2,1)S(1)} %copy.279), channel_id=1, replica_groups=mesh['grp'=2,'seq'=4,'ch'=2,'sub'=2] {'seq'}, dimensions={3} | all-to-all | bytes 786432 | tf_op jit(solution)/shard_map/all_to_all | solution.py:114
  195.1 3.5 all-to-all-start.5
  198.6 5.1 %convert_bitcast_fusion.1 = bf16[2,4,384,384]{2,3,0,1:T(8,128)(2,1)} fusion(bf16[2,4,384,512]{3,1,2,0:T(4,128)(2,1)} %copy-done.5, bf16[4,384,1,512]{3,0,2,1:T(4,128)(2,1)S(1)} %copy-done.6), kind=kOutput, calls=%fused_computation.29 | convolution fusion | flops 1209139200 | bytes 7077888 | tf_op jit(solution)/shard_map/gkqt,kpt->gkqp/dot_general | solution.py:88
  203.7 5.5 %all-to-all-done.5 = bf16[4,96,4,128]{3,1,0,2:T(8,128)(2,1)S(1)} async-done(((bf16[4,96,4,128]{3,1,0,2:T(8,128)(2,1)}), bf16[4,96,4,128]{3,1,0,2:T(8,128)(2,1)S(1)}, u32[]{:S(2)}, u32[]{:S(2)}) %all-to-all-start.5) | async-done | bytes 393248 | tf_op jit(solution)/shard_map/all_to_all | solution.py:124
  210.9 4.0 %fusion.39 = bf16[384,4,384]{0,2,1:T(8,128)(2,1)} fusion(bf16[4,384,512]{2,1,0:T(8,128)(2,1)} %get-tuple-element.46, bf16[4,384,512]{2,0,1:T(4,128)(2,1)} %all-gather.7.cloned.1.call-done), kind=kOutput, calls=%fused_computation.40 | convolution fusion | flops 604569600 | bytes 4325376 | tf_op jit(solution)/shard_map/jrt,jqt->rjq/dot_general | solution.py:81
  214.9 2.2 copy.257
  217.2 3.7 all-to-all-start.2
  220.9 1.9 fusion.55
  222.8 31.3 %psum.29 = bf16[128,4,4]{2,1,0:T(4,128)(2,1)S(1)} all-reduce(bf16[128,4,4]{2,1,0:T(4,128)(2,1)S(1)} %fusion.55), channel_id=1, replica_groups=mesh['grp'=2,'seq'=4,'ch'=2,'sub'=2] {'ch','sub'}, use_global_device_ids=true, to_apply=%region_3.0 | all-reduce | flops 2048 | bytes 8192 | tf_op jit(solution)/shard_map/psum | solution.py:121
  254.8 3.9 fusion.44
  259.7 3.5 all-to-all-start.3
  263.2 2.0 fusion.49
  266.9 2.1 convert_element_type.138
  269.0 116.8 %all-reduce.12.cloned.1.call-done = (bf16[2,4,384,384]{2,3,0,1:T(8,128)(2,1)}, bf16[384,4,384]{0,2,1:T(8,128)(2,1)}) async-done(((bf16[2,4,384,384]{2,3,0,1:T(8,128)(2,1)}, bf16[384,4,384]{0,2,1:T(8,128)(2,1)}), (bf16[2,4,384,384]{2,3,0,1:T(8,128)(2,1)}, bf16[384,4,384]{0,2,1:T(8,128)(2,1)})) %all-reduce.12.cloned.1.call-update) | async-done | bytes 3538960 | tf_op jit(solution)/shard_map/psum | solution.py:96
  385.8 4.5 %copy.293 = f32[2,4,384,384]{3,2,1,0:T(8,128)} copy(bf16[2,4,384,384]{2,3,0,1:T(8,128)(2,1)} %get-tuple-element.42) | data formatting | bytes 7077888
  390.3 3.6 copy.294
  (90 shorter events, 28.8 us)
Async XLA Ops:
  7.2 67.8 %copy-start = (bf16[2,4,384,384]{3,2,1,0:T(8,128)(2,1)S(1)}, bf16[2,4,384,384]{3,2,1,0:T(8,128)(2,1)}, u32[]{:S(2)}) copy-start(bf16[2,4,384,384]{3,2,1,0:T(8,128)(2,1)} %param.16) | copy-start | bytes 7077892
  7.2 9.1 %copy-start.20 = (bf16[128,4,4]{0,2,1:T(4,128)(2,1)S(1)}, bf16[128,4,4]{0,2,1:T(4,128)(2,1)}, u32[]{:S(2)}) copy-start(bf16[128,4,4]{0,2,1:T(4,128)(2,1)} %param.15) | copy-start | bytes 12292
  10.0 20.8 %all-to-all-start = ((bf16[4,96,1,512]{1,0,2,3:T(4,128)(2,1)}), bf16[4,96,1,512]{1,0,2,3:T(4,128)(2,1)S(1)}, u32[]{:S(2)}, u32[]{:S(2)}) async-start(bf16[4,96,1,512]{1,0,2,3:T(4,128)(2,1)} %copy.244), calls=%async_computation | async-start | bytes 1048576 | tf_op jit(solution)/shard_map/all_to_all | solution.py:32
  16.3 54.8 %all-gather.9.cloned.1.call-start = ((), (), s32[]{:S(2)}) async-start(), calls=%async_computation.9 | async-start | bytes 1966080 | tf_op jit(solution)/shard_map/all_gather | solution.py:49
  16.5 17.9 %copy-start.15 = (bf16[128,4,4,1]{1,2,3,0:T(4,128)(2,1)}, bf16[128,4,4,1]{1,2,3,0:T(4,128)(2,1)S(1)}, u32[]{:S(2)}) copy-start(bf16[128,4,4,1]{1,2,3,0:T(4,128)(2,1)S(1)} %copy.300) | copy-start | bytes 12292
  30.8 0.8 copy-start.9
  31.6 18.0 %copy-start.2 = (bf16[4,96,1,512]{3,1,2,0:T(8,128)(2,1)S(1)}, bf16[4,96,1,512]{3,1,2,0:T(8,128)(2,1)}, u32[]{:S(2)}) copy-start(bf16[4,96,1,512]{3,1,2,0:T(8,128)(2,1)} %param.11) | copy-start | bytes 1179652
  31.6 18.0 %copy-start.18 = (f32[4,96]{1,0:T(4,128)S(1)}, f32[4,96]{1,0:T(4,128)}, u32[]{:S(2)}) copy-start(f32[4,96]{1,0:T(4,128)} %param.13) | copy-start | bytes 4612
  31.6 18.0 %copy-start.19 = (f32[4,96]{1,0:T(4,128)S(1)}, f32[4,96]{1,0:T(4,128)}, u32[]{:S(2)}) copy-start(f32[4,96]{1,0:T(4,128)} %param.12) | copy-start | bytes 4612
  34.4 17.7 %copy-start.21 = (bf16[96,4,4]{0,2,1:T(4,128)(2,1)S(1)}, bf16[96,4,4]{0,2,1:T(4,128)(2,1)}, u32[]{:S(2)}) copy-start(bf16[96,4,4]{0,2,1:T(4,128)(2,1)} %param.20) | copy-start | bytes 9220
  52.1 49.7 %all-gather.7.cloned.1.call-start = ((), (), s32[]{:S(2)}) async-start(), calls=%async_computation.7 | async-start | bytes 1966080 | tf_op jit(solution)/shard_map/all_gather | solution.py:78
  52.4 2.2 copy-start.13
  54.6 116.5 %all-reduce.10.cloned.1.call-start = ((), (), s32[]{:S(2)}) async-start(), calls=%async_computation.10 | async-start | bytes 3145728
  88.8 9.2 %copy-start.17 = (f32[2,4,384]{2,1,0:T(4,128)S(1)}, f32[2,4,384]{2,1,0:T(4,128)}, u32[]{:S(2)}) copy-start(f32[2,4,384]{2,1,0:T(4,128)} %param.18) | copy-start | bytes 36868
  119.4 1.7 copy-start.5
  124.0 4.6 %copy-start.22 = (u32[32]{0:T(128)S(1)}, u32[32]{0:T(128)}, u32[]{:S(2)}) copy-start(u32[32]{0:T(128)} %constant.26) | copy-start | bytes 388
  124.0 49.0 %copy-start.3 = (bf16[4,96,1,512]{3,1,2,0:T(8,128)(2,1)S(1)}, bf16[4,96,1,512]{3,1,2,0:T(8,128)(2,1)}, u32[]{:S(2)}) copy-start(bf16[4,96,1,512]{3,1,2,0:T(8,128)(2,1)} %param.11) | copy-start | bytes 1179652
  124.0 49.0 %copy-start.14 = (bf16[4,96,1,512]{3,1,2,0:T(8,128)(2,1)S(1)}, bf16[4,96,1,512]{3,1,2,0:T(8,128)(2,1)}, u32[]{:S(2)}) copy-start(bf16[4,96,1,512]{3,1,2,0:T(8,128)(2,1)} %param.21) | copy-start | bytes 1179652
  128.0 65.4 %copy-start.16 = (bf16[128,4,4,1]{1,2,3,0:T(4,128)(2,1)S(1)}, bf16[128,4,4,1]{1,2,3,0:T(4,128)(2,1)}, u32[]{:S(2)}) copy-start(bf16[128,4,4,1]{1,2,3,0:T(4,128)(2,1)} %copy-done.15) | copy-start | bytes 12292
  128.0 126.8 %all-gather.5.cloned.1.call-start = ((), (), s32[]{:S(2)}) async-start(), calls=%async_computation.6 | async-start | bytes 5898240 | tf_op jit(solution)/shard_map/all_gather | solution.py:58
  173.4 25.3 %copy-start.6 = (bf16[4,384,1,512]{3,0,2,1:T(4,128)(2,1)S(1)}, bf16[4,384,1,512]{3,0,2,1:T(4,128)(2,1)}, u32[]{:S(2)}) copy-start(bf16[4,384,1,512]{3,0,2,1:T(4,128)(2,1)} %all-gather.9.cloned.1.call-done) | copy-start | bytes 4718596
  192.6 0.8 copy-start.11
  195.1 14.1 %all-to-all-start.5 = ((bf16[4,96,4,128]{3,1,0,2:T(8,128)(2,1)}), bf16[4,96,4,128]{3,1,0,2:T(8,128)(2,1)S(1)}, u32[]{:S(2)}, u32[]{:S(2)}) async-start(bf16[4,96,4,128]{3,1,0,2:T(8,128)(2,1)} %copy.283), calls=%async_computation.5 | async-start | bytes 786432 | tf_op jit(solution)/shard_map/all_to_all | solution.py:124
  198.6 68.3 %all-reduce.8.cloned.1.call-start = ((), (), s32[]{:S(2)}) async-start(), calls=%async_computation.8 | async-start | bytes 1048576 | tf_op jit(solution)/shard_map/psum | solution.py:131
  209.3 5.6 %copy-start.12 = (bf16[4,96,4,128]{3,1,0,2:T(8,128)(2,1)}, bf16[4,96,4,128]{3,1,0,2:T(8,128)(2,1)S(1)}, u32[]{:S(2)}) copy-start(bf16[4,96,4,128]{3,1,0,2:T(8,128)(2,1)S(1)} %all-to-all-done.5) | copy-start | bytes 1179652
  210.5 175.3 %all-reduce.12.cloned.1.call-start = ((), (), s32[]{:S(2)}) async-start(), calls=%async_computation.11 | async-start | bytes 7077888 | tf_op jit(solution)/shard_map/psum | solution.py:96
  210.8 4.1 %copy-start.7 = (bf16[4,384,512]{2,1,0:T(8,128)(2,1)S(1)}, bf16[4,384,512]{2,1,0:T(8,128)(2,1)}, u32[]{:S(2)}) copy-start(bf16[4,384,512]{2,1,0:T(8,128)(2,1)} %get-tuple-element.46) | copy-start | bytes 4718596
  217.2 3.7 copy-start.10
  217.2 37.7 %all-to-all-start.2 = ((bf16[4,384,512]{1,0,2:T(4,128)(2,1)}), bf16[4,384,512]{1,0,2:T(4,128)(2,1)S(1)}, u32[]{:S(2)}, u32[]{:S(2)}) async-start(bf16[4,384,512]{1,0,2:T(4,128)(2,1)} %copy.257), calls=%async_computation.2 | async-start | bytes 3145728 | tf_op jit(solution)/shard_map/all_to_all | solution.py:59
  254.8 8.3 %copy-start.4 = (f32[4,96,1,512]{3,1,0,2:T(8,128)S(1)}, f32[4,96,1,512]{3,1,0,2:T(8,128)}, u32[]{:S(2)}) copy-start(f32[4,96,1,512]{3,1,0,2:T(8,128)} %reshape.95) | copy-start | bytes 2359300
  259.7 134.3 %all-to-all-start.3 = ((bf16[384,4,128]{2,1,0:T(4,128)(2,1)}), bf16[384,4,128]{2,1,0:T(4,128)(2,1)S(1)}, u32[]{:S(2)}, u32[]{:S(2)}) async-start(bf16[384,4,128]{2,1,0:T(4,128)(2,1)} %copy.262), calls=%async_computation.3 | async-start | bytes 786432 | tf_op jit(solution)/shard_map/all_to_all | solution.py:67
  390.3 6.4 %copy-start.1 = (bf16[2,4,384,384]{3,2,1,0:T(8,128)(2,1)S(1)}, bf16[2,4,384,384]{3,2,1,0:T(8,128)(2,1)}, u32[]{:S(2)}) copy-start(bf16[2,4,384,384]{3,2,1,0:T(8,128)(2,1)} %param.16) | copy-start | bytes 7077892
  (1 other events, 0.7 us)
Sparse Core Ops, SparseCore 0:
  52.3 18.7 all-gather.8
  73.2 19.6 all-gather.6
  128.1 42.9 all-reduce.9
  172.6 37.5 all-gather.4
  212.9 36.6 all-reduce.7
  252.4 133.3 all-reduce.11
where the time goes:
time: 405 us; the launch traced here: 404 us
  waiting for transfers between devices  190 us (47%)
  blocking collectives  63.8 us (16%)
  matrix products  60.2 us (15%)
  local copies, waits for them, and re-layouts  47.4 us (12%)
  starting transfers between devices  17.6 us (4%)
  between operations  15.1 us (4%)
  other arithmetic  9.5 us (2%)
    psum x1, waiting for transfers between devices, per_device(): lax.psum(first_grad.astype(jnp.bfloat16), 'seq').astype(jnp.float32)  117 us
    unnamed x7, waiting for transfers between devices  41.9 us
    psum x1, blocking collectives, per_device(): lax.psum(left_factor_gradient.astype(jnp.bfloat16), ('ch', 'sub'))  31.3 us
    unnamed x56, local copies, waits for them, and re-layouts  21.4 us
    all_to_all x1, blocking collectives, per_device(): lax.all_to_all(mixed_tangent, 'seq', split_axis=3, concat_axis=2, tiled=T...  18.9 us
    all_to_all x1, waiting for transfers between devices, per_device(): lax.all_to_all(section_local, 'seq', split_axis=3, concat_axis=2, tiled=T...  14.3 us
    all_to_all x1, blocking collectives, per_device(): lax.all_to_all(mixed_spread, 'seq', split_axis=2, concat_axis=3, tiled=True)  13.6 us
    all_gather x1, waiting for transfers between devices, per_device(): lax.all_gather(flat_in, ('ch', 'sub'), axis=1, tiled=True)  11.5 us
  transfers between devices with their start and end apart: 10, of which 5 were waited for; matrix products, arithmetic and copies ran while one was open for 19% of the time, Pallas kernels for 0%

commit v1 on v0

v1 whole, which is shorter than its diff:
```python
import jax
import jax.numpy as jnp
from jax import lax
from jax.experimental import pallas as pl
from jax.experimental.pallas import tpu as pltpu
from jax.sharding import PartitionSpec as P

F32 = jnp.float32
BF16 = jnp.bfloat16
PLANE = ("ch", "sub")


def dot(a, b, dims):
    return lax.dot_general(a, b, (dims, ((), ())), preferred_element_type=F32)


def channel_kernel(
    x_ref, cot_ref, up_ref, down_ref, mix_ref, shift_ref,
    back_ref, reduced_ref, up_grad_ref, down_grad_ref,
    x_all, cot_all, back_acc, reduced_acc,
):
    step = pl.program_id(0)
    shares, blocks, part = x_ref.shape[:3]

    @pl.when(step == 0)
    def _():
        for d in range(shares):
            x_all[:, d * part:(d + 1) * part, :] = x_ref[d]
            cot_all[:, d * part:(d + 1) * part, :] = cot_ref[d]
        back_acc[...] = jnp.zeros_like(back_acc)
        reduced_acc[...] = jnp.zeros_like(reduced_acc)

    def mix(g, j, k):
        col = (g * blocks + j) * blocks + k
        return mix_ref[:, col:col + 1]

    stacked = []
    for g in range(2):
        lifted = [dot(up_ref[g, k], x_all[k], ((1,), (0,))) for k in range(blocks)]
        rows = []
        for j in range(blocks):
            total = shift_ref[:, g * blocks + j:g * blocks + j + 1] + mix(g, j, 0) * lifted[0]
            for k in range(1, blocks):
                total = total + mix(g, j, k) * lifted[k]
            rows.append(total)
        stacked.append(rows)
    cots = [[], []]
    root = 0.7978845608028654
    for j in range(blocks):
        s0, s1 = stacked[0][j], stacked[1][j]
        square = s0 * s0
        t = jnp.tanh(root * (s0 + 0.044715 * (square * s0)))
        half = 0.5 * (1.0 + t)
        gelu = s0 * half
        slope = half + (0.5 * root) * s0 * (1.0 - t * t) * (1.0 + 3 * 0.044715 * square)
        hidden = (gelu * s1).astype(BF16)
        reduced_acc[j] += dot(down_ref[j], hidden, ((0,), (0,)))
        down_grad_ref[j] = dot(cot_all[j], hidden, ((1,), (1,))).astype(BF16)
        hidden_cot = dot(down_ref[j], cot_all[j], ((1,), (0,)))
        cots[0].append(hidden_cot * s1 * slope)
        cots[1].append(hidden_cot * gelu)
    for k in range(blocks):
        for g in range(2):
            total = mix(g, 0, k) * cots[g][0]
            for j in range(1, blocks):
                total = total + mix(g, j, k) * cots[g][j]
            lifted_cot = total.astype(BF16)
            back_acc[k] += dot(up_ref[g, k], lifted_cot, ((0,), (0,)))
            up_grad_ref[g, k] = dot(lifted_cot, x_all[k], ((1,), (1,))).astype(BF16)

    @pl.when(step == pl.num_programs(0) - 1)
    def _():
        for d in range(shares):
            back_ref[d] = back_acc[:, d * part:(d + 1) * part, :].astype(BF16)
            reduced_ref[d] = reduced_acc[:, d * part:(d + 1) * part, :].astype(BF16)


def channel_block(x, cot, up_first, up_second, up_shift, down_first):
    shares, blocks, part, tokens = x.shape
    chans = shares * part
    hidden = up_first.shape[2]
    if part % 16:
        x = jnp.swapaxes(x, 0, 1).reshape(1, blocks, chans, tokens)
        cot = jnp.swapaxes(cot, 0, 1).reshape(1, blocks, chans, tokens)
    tile = 128 if hidden % 128 == 0 else hidden
    down = jnp.transpose(down_first, (1, 2, 0))
    mix = jnp.transpose(up_second, (1, 0, 2, 3)).reshape(hidden, 2 * blocks * blocks).astype(F32)
    shift = jnp.transpose(up_shift, (2, 0, 1)).reshape(hidden, 2 * blocks)
    whole = pl.BlockSpec(x.shape, lambda i: (0, 0, 0, 0))
    back, reduced, up_grad, down_grad = pl.pallas_call(
        channel_kernel,
        grid=(hidden // tile,),
        in_specs=[
            whole,
            whole,
            pl.BlockSpec((2, blocks, tile, chans), lambda i: (0, 0, i, 0)),
            pl.BlockSpec((blocks, tile, chans), lambda i: (0, i, 0)),
            pl.BlockSpec((tile, 2 * blocks * blocks), lambda i: (i, 0)),
            pl.BlockSpec((tile, 2 * blocks), lambda i: (i, 0)),
        ],
        out_specs=[
            whole,
            whole,
            pl.BlockSpec((2, blocks, tile, chans), lambda i: (0, 0, i, 0)),
            pl.BlockSpec((blocks, chans, tile), lambda i: (0, 0, i)),
        ],
        out_shape=[
            jax.ShapeDtypeStruct(x.shape, BF16),
            jax.ShapeDtypeStruct(x.shape, BF16),
            jax.ShapeDtypeStruct((2, blocks, hidden, chans), BF16),
            jax.ShapeDtypeStruct((blocks, chans, hidden), BF16),
        ],
        scratch_shapes=[
            pltpu.VMEM((blocks, chans, tokens), BF16),
            pltpu.VMEM((blocks, chans, tokens), BF16),
            pltpu.VMEM((blocks, chans, tokens), F32),
            pltpu.VMEM((blocks, chans, tokens), F32),
        ],
        compiler_params=pltpu.CompilerParams(
            dimension_semantics=("arbitrary",), vmem_limit_bytes=50 * 1024 * 1024
        ),
        cost_estimate=pl.CostEstimate(
            flops=18 * blocks * hidden * chans * tokens,
            bytes_accessed=14 * 1024 * 1024,
            transcendentals=blocks * hidden * tokens,
        ),
    )(x, cot, up_first, down, mix, shift)
    if part % 16:
        back = jnp.swapaxes(back.reshape(blocks, shares, part, tokens), 0, 1)
        reduced = jnp.swapaxes(reduced.reshape(blocks, shares, part, tokens), 0, 1)
    return back, reduced, up_grad, down_grad


def pieces_sum(x, axes):
    moved = lax.all_to_all(x, axes, split_axis=0, concat_axis=0, tiled=True)
    return jnp.sum(moved.astype(F32), axis=0)


def ring_sum(x, axis, way):
    n = lax.axis_size(axis)
    me = lax.axis_index(axis)
    perm = [(i, (i + way) % n) for i in range(n)]
    rows = x.reshape(n, -1, x.shape[-1])

    def own(back):
        return lax.dynamic_index_in_dim(rows, (me - way * back) % n, 0, keepdims=False)

    held = own(1)
    for s in range(n - 1):
        held = (lax.ppermute(held, axis, perm).astype(F32) + own(s + 2).astype(F32)).astype(BF16)
    out = jnp.zeros(rows.shape, F32)
    out = lax.dynamic_update_index_in_dim(out, held.astype(F32), me, 0)
    for s in range(n - 1):
        held = lax.ppermute(held, axis, perm)
        out = lax.dynamic_update_index_in_dim(out, held.astype(F32), (me - way * (s + 1)) % n, 0)
    return out.reshape(x.shape)


def swap_sum(x):
    for axis in ("sub", "ch"):
        n = lax.axis_size(axis)
        bit = 1
        while bit < n:
            sent = x.astype(BF16)
            got = lax.ppermute(sent, axis, [(i, i ^ bit) for i in range(n)])
            x = sent.astype(F32) + got.astype(F32)
            bit *= 2
    return x


def per_device(
    tokens,
    gate_scale,
    gate_shift,
    sequence_right_factor,
    sequence_left_factor,
    up_first,
    up_second,
    up_shift,
    down_first,
    down_second,
    cotangent,
):
    blocks, part, _, length = tokens.shape
    rows = blocks * part
    n = lax.axis_size("seq")
    step = length // n
    right = sequence_right_factor[0]
    left = jnp.transpose(sequence_left_factor, (1, 2, 0)).astype(F32)
    flat = tokens.reshape(rows, length)
    upstream = cotangent.reshape(blocks, part, length)

    def to_positions(x):
        x = jnp.swapaxes(x.reshape(rows, n, step), 0, 1)
        return lax.all_to_all(x, "seq", split_axis=0, concat_axis=0, tiled=True)

    def to_blocks(x):
        x = lax.all_to_all(x, "seq", split_axis=0, concat_axis=0, tiled=True)
        return jnp.swapaxes(x, 0, 1).reshape(rows, length)

    section = dot(flat, right, ((1,), (1,))).astype(BF16)
    sections = to_positions(section)
    second = down_second.astype(F32)
    down_cot = jnp.stack(
        [
            sum(second[:, k, j, None] * upstream[k].astype(F32) for k in range(blocks))
            for j in range(blocks)
        ]
    ).astype(BF16)
    cot_all = lax.all_gather(down_cot, PLANE, axis=0)
    mixed = jnp.sum(left[:, :, None, :] * sections.astype(F32)[None], axis=1).astype(BF16)
    mixed_float = to_blocks(mixed).astype(F32)
    scale = gate_scale.reshape(rows, 1)
    shift = gate_shift.reshape(rows, 1)
    input_tokens = flat.astype(F32)
    gating = jax.nn.sigmoid(input_tokens * scale + shift)
    seq_out = (input_tokens + gating * mixed_float).astype(BF16)
    block_in = seq_out.reshape(blocks, part, length)
    x_all = lax.all_gather(block_in, PLANE, axis=0)
    back, reduced, up_grad, down_grad = channel_block(
        x_all, cot_all, up_first, up_second, up_shift, down_first
    )
    up_first_grad = ring_sum(up_grad, "seq", 1)
    down_first_grad = jnp.swapaxes(ring_sum(down_grad, "seq", -1), 0, 1)

    input_cot = pieces_sum(back, PLANE).reshape(rows, length)
    total_cot = cotangent.reshape(rows, length).astype(F32) + input_cot
    mixed_cot = (total_cot * gating).astype(BF16)
    straight = total_cot + total_cot * mixed_float * gating * (1.0 - gating) * scale
    cots = to_positions(mixed_cot).astype(F32)
    section_spread = jnp.sum(left[:, :, None, :] * cots[:, None], axis=0).astype(BF16)
    left_grad = jnp.sum(cots[:, None] * sections.astype(F32)[None], axis=2)
    section_cot = to_blocks(section_spread)
    right_grad = dot(section_cot, flat, ((0,), (0,)))
    token_grad = straight + dot(section_cot, right, ((1,), (0,)))

    sums = pieces_sum(reduced, PLANE)
    layer_out = jnp.stack(
        [
            block_in[k].astype(F32)
            + sum(second[:, k, j, None] * sums[j] for j in range(blocks))
            for k in range(blocks)
        ]
    ).astype(BF16)
    left_grad = jnp.transpose(swap_sum(left_grad), (2, 0, 1))
    right_grad = swap_sum(right_grad)
    return (
        layer_out.reshape(tokens.shape),
        token_grad.reshape(tokens.shape),
        right_grad[None],
        left_grad,
        up_first_grad,
        down_first_grad,
    )


def solution(mesh):
    placed = (
        P("grp", PLANE, "seq", None),
        P(None, PLANE),
        P(None, PLANE),
        P("seq", None, None),
        P("seq", None, None),
        P(None, None, PLANE, None),
        P(None, PLANE, None, None),
        P(None, None, PLANE),
        P(None, None, PLANE),
        P(PLANE, None, None),
        P("grp", PLANE, "seq", None),
    )
    return jax.shard_map(
        per_device,
        mesh=mesh,
        in_specs=placed,
        out_specs=(
            P("grp", PLANE, "seq", None),
            P("grp", PLANE, "seq", None),
            P(("grp", "seq"), None, None),
            P(("grp", "seq"), None, None),
            P("grp", None, PLANE, None),
            P("grp", None, PLANE),
        ),
        check_vma=False,
    )
```

time: 405 us -> 291 us (0.72)
  waiting for transfers between devices: 190 us -> 77.9 us
  matrix products: 60.2 us -> 2.26 us
  blocking collectives: 63.8 us -> 13.3 us
  other arithmetic: 9.5 us -> 42.1 us
  starting transfers between devices: 17.6 us -> 48.9 us
  local copies, waits for them, and re-layouts: 47.4 us -> 70.6 us
  Pallas kernels: 0 us -> 18.5 us
    psum x2 -> x0, waiting for transfers between devices: 117 us -> none  [the longest x1 117 us: per_device(): lax.psum(first_grad.astype(jnp.bfloat16), 'seq').astype(jnp.float32)]
    dot_general x16 -> x3, matrix products: 60.2 us -> 2.26 us  [dot(): return lax.dot_general(a, b, (dims, ((), ())), preferred_element_type=F32)]
    dynamic_update_slice x0 -> x4, local copies, waits for them, and re-layouts: none -> 51.1 us  [the longest x3 38.4 us: ring_sum(): lax.dynamic_update_index_in_dim(out, held.astype(F32), (me - way * (s + 1...]
    ppermute x0 -> x16, waiting for transfers between devices: none -> 50.2 us  [the longest x6 25.8 us: ring_sum(): lax.ppermute(held, axis, perm).astype(F32) + own(s + 2).astype(F32)]
    unnamed x7 -> x2, waiting for transfers between devices: 41.9 us -> 0.03 us
    psum x1 -> x0, blocking collectives: 31.3 us -> none  [per_device(): lax.psum(left_factor_gradient.astype(jnp.bfloat16), ('ch', 'sub'))]
    ppermute x0 -> x16, starting transfers between devices: none -> 25.1 us  [the longest x6 10.8 us: ring_sum(): held = lax.ppermute(held, axis, perm)]
    all_to_all x2 -> x1, blocking collectives: 32.5 us -> 13.3 us  [to_blocks(): x = lax.all_to_all(x, 'seq', split_axis=0, concat_axis=0, tiled=True)]
  transfers between devices with their start and end apart: 10 -> 23, of which waited for: 5 -> 7; matrix products, arithmetic and copies ran while one was open for 19% -> 37% of each run, Pallas kernels for 0% -> 0%
where the time goes in v1:
time: 291 us; the launch traced here: 288 us
  waiting for transfers between devices  77.9 us (27%)
  local copies, waits for them, and re-layouts  70.6 us (24%)
  starting transfers between devices  48.9 us (17%)
  other arithmetic  42.1 us (14%)
  Pallas kernels  18.5 us (6%)
  between operations  14.5 us (5%)
  blocking collectives  13.3 us (5%)
    dynamic_update_slice x3, local copies, waits for them, and re-layouts, ring_sum(): lax.dynamic_update_index_in_dim(out, held.astype(F32), (me - way * (s + 1...  38.4 us
    ppermute x6, waiting for transfers between devices, ring_sum(): lax.ppermute(held, axis, perm).astype(F32) + own(s + 2).astype(F32)  25.8 us
    ppermute x6, waiting for transfers between devices, ring_sum(): held = lax.ppermute(held, axis, perm)  24.4 us
    pallas_call x1, Pallas kernels, channel_block(): pl.pallas_call(channel_kernel, grid=(hidden // tile,), in_specs=[whole, w...  18.5 us
    all_gather x1, waiting for transfers between devices, per_device(): x_all = lax.all_gather(block_in, PLANE, axis=0)  16 us
    all_to_all x1, blocking collectives, to_blocks(): x = lax.all_to_all(x, 'seq', split_axis=0, concat_axis=0, tiled=True)  13.3 us
    dynamic_update_slice x1, local copies, waits for them, and re-layouts, ring_sum(): out = lax.dynamic_update_index_in_dim(out, held.astype(F32), me, 0)  12.8 us
    all_to_all x2, waiting for transfers between devices, to_positions(): return lax.all_to_all(x, 'seq', split_axis=0, concat_axis=0, tiled=True)  11.7 us
  transfers between devices with their start and end apart: 23, of which 7 were waited for; matrix products, arithmetic and copies ran while one was open for 37% of the time, Pallas kernels for 0%

profile of v1, /device:TPU:0, one launch (start us, length us, event | category | flops | bytes accessed | tf_op | source)
XLA Modules:
  0.0 288.0 jit_solution(11693486857186068695)
XLA Ops:
  12.6 6.3 %all-to-all-start = ((bf16[4,384,128]{2,1,0:T(8,128)(2,1)}), bf16[4,384,128]{2,1,0:T(8,128)(2,1)S(1)}, u32[]{:S(2)}, u32[]{:S(2)}) async-start(bf16[4,384,128]{2,1,0:T(8,128)(2,1)} %bitcast.242), calls=%async_computation | async-start | bytes 786432 | tf_op jit(solution)/shard_map/all_to_all | solution.py:195
  19.0 11.7 %all-to-all-done = bf16[4,384,128]{2,1,0:T(8,128)(2,1)S(1)} async-done(((bf16[4,384,128]{2,1,0:T(8,128)(2,1)}), bf16[4,384,128]{2,1,0:T(8,128)(2,1)S(1)}, u32[]{:S(2)}, u32[]{:S(2)}) %all-to-all-start) | async-done | bytes 393248 | tf_op jit(solution)/shard_map/all_to_all | solution.py:195
  31.8 13.3 %all_to_all.30 = bf16[4,384,128]{2,1,0:T(8,128)(2,1)S(1)} all-to-all(bf16[4,384,128]{2,1,0:T(8,128)(2,1)S(1)} %multiply_reduce_fusion.2), channel_id=1, replica_groups=mesh['grp'=2,'seq'=4,'ch'=2,'sub'=2] {'seq'}, dimensions={0} | all-to-all | bytes 786432 | tf_op jit(solution)/shard_map/all_to_all | solution.py:198
  48.2 2.5 copy.68
  51.1 16.0 %all-gather.3.cloned.1.call-done.x_ref = bf16[4,4,96,512]{3,2,1,0:T(8,128)(2,1)} async-done(((bf16[1,4,96,512]{3,2,1,0:T(8,128)(2,1)}), bf16[4,4,96,512]{3,2,1,0:T(8,128)(2,1)}) %all-gather.3.cloned.1.call-update) | async-done | bytes 1572880 | tf_op jit(solution)/shard_map/all_gather | solution.py:219
  67.1 18.5 %shard_map.154 = (bf16[4,4,96,512]{3,2,1,0:T(8,128)(2,1)}, bf16[4,4,96,512]{3,2,1,0:T(8,128)(2,1)}, bf16[2,4,384,384]{3,2,1,0:T(8,128)(2,1)}, bf16[4,384,384]{2,1,0:T(8,128)(2,1)S(1)}) custom-call(bf16[4,4,96,512]{3,2,1,0:T(8,128)(2,1)} %all-gather.3.cloned.1.call-done.x_ref, bf16[4,4,96,512]{3,2,1,0:T(8,128)(2,1)} %all-gather.5.cloned.1.call-done.cot_ref, ...), custom_call_target="tpu_custom_call" | custom-call | flops 5435817984 | bytes 14680064 | tf_op jit(solution)/shard_map/pallas_call | solution.py:90
  88.2 2.4 collective-permute-start.10
  90.6 4.3 %all-to-all-start.2 = ((bf16[4,4,96,512]{3,2,1,0:T(8,128)(2,1)}), bf16[4,4,96,512]{3,2,1,0:T(8,128)(2,1)}, u32[]{:S(2)}, u32[]{:S(2)}) async-start(bf16[4,4,96,512]{3,2,1,0:T(8,128)(2,1)} %get-tuple-element.10), calls=%async_computation.2 | async-start | bytes 3145728 | tf_op jit(solution)/shard_map/all_to_all | solution.py:135
  95.0 14.9 %collective-permute-done.10 = bf16[384,384]{1,0:T(8,128)(2,1)} collective-permute-done((bf16[384,384]{1,0:T(8,128)(2,1)S(1)}, bf16[384,384]{1,0:T(8,128)(2,1)}, u32[]{:S(2)}, u32[]{:S(2)}) %collective-permute-start.10) | collective-permute-done | bytes 294944 | tf_op jit(solution)/shard_map/ppermute | solution.py:150
  110.9 2.1 collective-permute-start.11
  113.0 2.2 fusion.3
  115.3 5.3 %collective-permute-done.11 = bf16[384,384]{1,0:T(8,128)(2,1)} collective-permute-done((bf16[384,384]{1,0:T(8,128)(2,1)S(1)}, bf16[384,384]{1,0:T(8,128)(2,1)}, u32[]{:S(2)}, u32[]{:S(2)}) %collective-permute-start.11) | collective-permute-done | bytes 294944 | tf_op jit(solution)/shard_map/ppermute | solution.py:150
  122.3 4.4 %collective-permute-start.12 = (bf16[384,384]{1,0:T(8,128)(2,1)}, bf16[384,384]{1,0:T(8,128)(2,1)}, u32[]{:S(2)}, u32[]{:S(2)}) collective-permute-start(bf16[384,384]{1,0:T(8,128)(2,1)} %fusion.23), channel_id=1, source_target_pairs={{0,12},{4,0},{8,4},{12,8},{1,13},{5,1},{9,5},{13,9},{2,14},{6,2},{... | collective-permute-start | bytes 884744 | tf_op jit(solution)/shard_map/ppermute | solution.py:150
  129.2 4.7 %all-to-all-start.3 = ((bf16[4,4,96,512]{3,2,1,0:T(8,128)(2,1)}), bf16[4,4,96,512]{3,2,1,0:T(8,128)(2,1)}, u32[]{:S(2)}, u32[]{:S(2)}) async-start(bf16[4,4,96,512]{3,2,1,0:T(8,128)(2,1)} %get-tuple-element.11), calls=%async_computation.3 | async-start | bytes 3145728 | tf_op jit(solution)/shard_map/all_to_all | solution.py:135
  135.0 5.7 %collective-permute-done.12 = bf16[384,384]{1,0:T(8,128)(2,1)} collective-permute-done((bf16[384,384]{1,0:T(8,128)(2,1)}, bf16[384,384]{1,0:T(8,128)(2,1)}, u32[]{:S(2)}, u32[]{:S(2)}) %collective-permute-start.12) | collective-permute-done | bytes 294944 | tf_op jit(solution)/shard_map/ppermute | solution.py:150
  143.1 3.2 %collective-permute-start.13 = (bf16[384,384]{1,0:T(8,128)(2,1)}, bf16[384,384]{1,0:T(8,128)(2,1)}, u32[]{:S(2)}, u32[]{:S(2)}) collective-permute-start(bf16[384,384]{1,0:T(8,128)(2,1)} %get-tuple-element.47), channel_id=1, source_target_pairs={{0,12},{4,0},{8,4},{12,8},{1,13},{5,1},{9,5},{13,9},{2,14},{6,2},{... | collective-permute-start | bytes 884744 | tf_op jit(solution)/shard_map/ppermute | solution.py:154
  148.0 12.8 %dynamic_update_slice.30 = f32[4,384,384]{2,0,1:T(4,128)} dynamic-update-slice(f32[4,384,384]{2,0,1:T(4,128)} %broadcast_in_dim.75, f32[1,384,384]{2,0,1:T(1,128)S(1)} %copy.73, s32[]{:T(128)S(6)} %select_n.93, s32[]{:T(128)} %constant.117.clone.1, s32[]{:T(128)} %constant.117.clone.1) | dynamic-update-slice | bytes 1179652 | tf_op jit(solution)/shard_map/jit(dynamic_update_index_in_dim)/dynamic_update_slice | solution.py:152
  160.8 2.3 fusion.2
  168.9 2.7 fusion.27
  172.5 4.9 %all-to-all-start.4 = ((bf16[4,384,128]{2,1,0:T(8,128)(2,1)}), bf16[4,384,128]{2,1,0:T(8,128)(2,1)}, u32[]{:S(2)}, u32[]{:S(2)}) async-start(bf16[4,384,128]{2,1,0:T(8,128)(2,1)} %copy.71), calls=%async_computation.4 | async-start | bytes 786432 | tf_op jit(solution)/shard_map/all_to_all | solution.py:195
  180.1 3.8 %collective-permute-start.14 = (bf16[384,384]{1,0:T(8,128)(2,1)}, bf16[384,384]{1,0:T(8,128)(2,1)}, u32[]{:S(2)}, u32[]{:S(2)}) collective-permute-start(bf16[384,384]{1,0:T(8,128)(2,1)} %collective-permute-done.13), channel_id=1, source_target_pairs={{0,12},{4,0},{8,4},{12,8},{1,13},{5,1},{9,5},{13,9},{2,14},{6,2},{... | collective-permute-start | bytes 884744 | tf_op jit(solution)/shard_map/ppermute | solution.py:154
  185.6 12.8 %dynamic_update_slice.31 = f32[4,384,384]{2,0,1:T(4,128)} dynamic-update-slice(f32[4,384,384]{2,0,1:T(4,128)} %dynamic_update_slice.30, f32[1,384,384]{2,0,1:T(1,128)S(1)} %copy.74, s32[]{:T(128)S(6)} %select_n.95, s32[]{:T(128)} %constant.117.clone.1, s32[]{:T(128)} %constant.117.clone.1) | dynamic-update-slice | bytes 1179652 | tf_op jit(solution)/shard_map/jit(dynamic_update_index_in_dim)/dynamic_update_slice | solution.py:155
  200.7 3.5 %all-to-all-start.5 = ((bf16[4,384,128]{2,1,0:T(8,128)(2,1)}), bf16[4,384,128]{2,1,0:T(8,128)(2,1)S(1)}, u32[]{:S(2)}, u32[]{:S(2)}) async-start(bf16[4,384,128]{2,1,0:T(8,128)(2,1)} %get-tuple-element.45), calls=%async_computation.5 | async-start | bytes 786432 | tf_op jit(solution)/shard_map/all_to_all | solution.py:198
  205.8 12.8 %dynamic_update_slice.32 = f32[4,384,384]{2,0,1:T(4,128)} dynamic-update-slice(f32[4,384,384]{2,0,1:T(4,128)} %dynamic_update_slice.31, f32[1,384,384]{2,0,1:T(1,128)S(1)} %copy.75, s32[]{:T(128)S(6)} %select_n.97, s32[]{:T(128)} %constant.117.clone.1, s32[]{:T(128)} %constant.117.clone.1) | dynamic-update-slice | bytes 1179652 | tf_op jit(solution)/shard_map/jit(dynamic_update_index_in_dim)/dynamic_update_slice | solution.py:155
  218.6 3.8 %collective-permute-start.15 = (bf16[384,384]{1,0:T(8,128)(2,1)}, bf16[384,384]{1,0:T(8,128)(2,1)}, u32[]{:S(2)}, u32[]{:S(2)}) collective-permute-start(bf16[384,384]{1,0:T(8,128)(2,1)} %collective-permute-done.14), channel_id=1, source_target_pairs={{0,12},{4,0},{8,4},{12,8},{1,13},{5,1},{9,5},{13,9},{2,14},{6,2},{... | collective-permute-start | bytes 884744 | tf_op jit(solution)/shard_map/ppermute | solution.py:154
  222.3 2.5 broadcast_in_dim.66
  224.8 2.6 convert_dynamic-update-slice_fusion.3
  227.4 1.9 collective-permute-start.3
  232.7 12.8 %dynamic_update_slice.33 = f32[4,384,384]{2,0,1:T(4,128)} dynamic-update-slice(f32[4,384,384]{2,0,1:T(4,128)} %dynamic_update_slice.32, f32[1,384,384]{2,0,1:T(1,128)S(1)} %copy.76, s32[]{:T(128)S(6)} %select_n.99, s32[]{:T(128)} %constant.117.clone.1, s32[]{:T(128)} %constant.117.clone.1) | dynamic-update-slice | bytes 1179652 | tf_op jit(solution)/shard_map/jit(dynamic_update_index_in_dim)/dynamic_update_slice | solution.py:155
  246.1 2.2 convert_dynamic-update-slice_fusion.2
  251.2 12.1 %collective-permute-done.8 = bf16[768,384]{1,0:T(8,128)(2,1)S(1)} collective-permute-done((bf16[768,384]{1,0:T(8,128)(2,1)}, bf16[768,384]{1,0:T(8,128)(2,1)S(1)}, u32[]{:S(2)}, u32[]{:S(2)}) %collective-permute-start.8) | collective-permute-done | bytes 589856 | tf_op jit(solution)/shard_map/ppermute | solution.py:154
  267.8 12.3 %collective-permute-done.9 = bf16[768,384]{1,0:T(8,128)(2,1)S(1)} collective-permute-done((bf16[768,384]{1,0:T(8,128)(2,1)S(1)}, bf16[768,384]{1,0:T(8,128)(2,1)S(1)}, u32[]{:S(2)}, u32[]{:S(2)}) %collective-permute-start.9) | collective-permute-done | bytes 589856 | tf_op jit(solution)/shard_map/ppermute | solution.py:154
  (119 shorter events, 50.5 us)
Async XLA Ops:
  7.2 4.2 %copy-start = (bf16[1,512,512]{2,1,0:T(8,128)(2,1)S(1)}, bf16[1,512,512]{2,1,0:T(8,128)(2,1)}, u32[]{:S(2)}) copy-start(bf16[1,512,512]{2,1,0:T(8,128)(2,1)} %param.14) | copy-start | bytes 1572868
  7.2 4.2 %copy-start.1 = (bf16[4,96,1,512]{3,1,2,0:T(8,128)(2,1)S(1)}, bf16[4,96,1,512]{3,1,2,0:T(8,128)(2,1)}, u32[]{:S(2)}) copy-start(bf16[4,96,1,512]{3,1,2,0:T(8,128)(2,1)} %param.11) | copy-start | bytes 1179652
  7.2 43.9 %all-gather.5.cloned.1.call-start = ((), (), s32[]{:S(2)}) async-start(), calls=%async_computation.7 | async-start | bytes 1966080 | tf_op jit(solution)/shard_map/all_gather | solution.py:210
  9.3 9.7 %copy-start.15 = (bf16[128,4,4]{0,2,1:T(4,128)(2,1)S(1)}, bf16[128,4,4]{0,2,1:T(4,128)(2,1)}, u32[]{:S(2)}) copy-start(bf16[128,4,4]{0,2,1:T(4,128)(2,1)} %param.15) | copy-start | bytes 12292
  12.6 18.0 %all-to-all-start = ((bf16[4,384,128]{2,1,0:T(8,128)(2,1)}), bf16[4,384,128]{2,1,0:T(8,128)(2,1)S(1)}, u32[]{:S(2)}, u32[]{:S(2)}) async-start(bf16[4,384,128]{2,1,0:T(8,128)(2,1)} %bitcast.242), calls=%async_computation | async-start | bytes 786432 | tf_op jit(solution)/shard_map/all_to_all | solution.py:195
  18.9 48.1 %all-gather.3.cloned.1.call-start = ((), (), s32[]{:S(2)}) async-start(), calls=%async_computation.6 | async-start | bytes 1966080 | tf_op jit(solution)/shard_map/all_gather | solution.py:219
  86.7 26.4 %collective-permute-start.4 = (bf16[768,384]{1,0:T(8,128)(2,1)S(1)}, bf16[768,384]{1,0:T(8,128)(2,1)}, u32[]{:S(2)}, u32[]{:S(2)}) collective-permute-start(bf16[768,384]{1,0:T(8,128)(2,1)S(1)} %dynamic-slice_bitcast_fusion), channel_id=1, source_target_pairs={{0,4},{4,8},{8,12},{12,0},{1,5},{5,9},{9,13},{13,1},{2,6},{6,10},{... | collective-permute-start | bytes 1769480 | tf_op jit(solution)/shard_map/ppermute | solution.py:150
  88.2 21.7 %collective-permute-start.10 = (bf16[384,384]{1,0:T(8,128)(2,1)S(1)}, bf16[384,384]{1,0:T(8,128)(2,1)}, u32[]{:S(2)}, u32[]{:S(2)}) collective-permute-start(bf16[384,384]{1,0:T(8,128)(2,1)S(1)} %dynamic-slice_bitcast_fusion.1), channel_id=1, source_target_pairs={{0,12},{4,0},{8,4},{12,8},{1,13},{5,1},{9,5},{13,9},{2,14},{6,2},{... | collective-permute-start | bytes 884744 | tf_op jit(solution)/shard_map/ppermute | solution.py:150
  90.6 38.6 %all-to-all-start.2 = ((bf16[4,4,96,512]{3,2,1,0:T(8,128)(2,1)}), bf16[4,4,96,512]{3,2,1,0:T(8,128)(2,1)}, u32[]{:S(2)}, u32[]{:S(2)}) async-start(bf16[4,4,96,512]{3,2,1,0:T(8,128)(2,1)} %get-tuple-element.10), calls=%async_computation.2 | async-start | bytes 3145728 | tf_op jit(solution)/shard_map/all_to_all | solution.py:135
  95.0 31.7 %copy-start.2 = (bf16[4,96,1,512]{3,1,2,0:T(8,128)(2,1)S(1)}, bf16[4,96,1,512]{3,1,2,0:T(8,128)(2,1)}, u32[]{:S(2)}) copy-start(bf16[4,96,1,512]{3,1,2,0:T(8,128)(2,1)} %param.11) | copy-start | bytes 1179652
  95.0 31.9 %copy-start.5 = (bf16[4,96,1,512]{3,1,2,0:T(8,128)(2,1)S(1)}, bf16[4,96,1,512]{3,1,2,0:T(8,128)(2,1)}, u32[]{:S(2)}) copy-start(bf16[4,96,1,512]{3,1,2,0:T(8,128)(2,1)} %param.21) | copy-start | bytes 1179652
  110.9 9.6 %collective-permute-start.11 = (bf16[384,384]{1,0:T(8,128)(2,1)S(1)}, bf16[384,384]{1,0:T(8,128)(2,1)}, u32[]{:S(2)}, u32[]{:S(2)}) collective-permute-start(bf16[384,384]{1,0:T(8,128)(2,1)S(1)} %fusion.24), channel_id=1, source_target_pairs={{0,12},{4,0},{8,4},{12,8},{1,13},{5,1},{9,5},{13,9},{2,14},{6,2},{... | collective-permute-start | bytes 884744 | tf_op jit(solution)/shard_map/ppermute | solution.py:150
  115.3 45.5 %collective-permute-start.5 = (bf16[768,384]{1,0:T(8,128)(2,1)}, bf16[768,384]{1,0:T(8,128)(2,1)}, u32[]{:S(2)}, u32[]{:S(2)}) collective-permute-start(bf16[768,384]{1,0:T(8,128)(2,1)} %fusion.3), channel_id=1, source_target_pairs={{0,4},{4,8},{8,12},{12,0},{1,5},{5,9},{9,13},{13,1},{2,6},{6,10},{... | collective-permute-start | bytes 1769480 | tf_op jit(solution)/shard_map/ppermute | solution.py:150
  122.3 18.4 %collective-permute-start.12 = (bf16[384,384]{1,0:T(8,128)(2,1)}, bf16[384,384]{1,0:T(8,128)(2,1)}, u32[]{:S(2)}, u32[]{:S(2)}) collective-permute-start(bf16[384,384]{1,0:T(8,128)(2,1)} %fusion.23), channel_id=1, source_target_pairs={{0,12},{4,0},{8,4},{12,8},{1,13},{5,1},{9,5},{13,9},{2,14},{6,2},{... | collective-permute-start | bytes 884744 | tf_op jit(solution)/shard_map/ppermute | solution.py:150
  129.2 4.7 %copy-start.6 = (f32[4,48,8,128]{3,2,1,0:T(8,128)S(1)}, f32[4,48,8,128]{3,2,1,0:T(8,128)}, u32[]{:S(2)}) copy-start(f32[4,48,8,128]{3,2,1,0:T(8,128)} %get-tuple-element.54) | copy-start | bytes 2359300
  129.2 36.8 %all-to-all-start.3 = ((bf16[4,4,96,512]{3,2,1,0:T(8,128)(2,1)}), bf16[4,4,96,512]{3,2,1,0:T(8,128)(2,1)}, u32[]{:S(2)}, u32[]{:S(2)}) async-start(bf16[4,4,96,512]{3,2,1,0:T(8,128)(2,1)} %get-tuple-element.11), calls=%async_computation.3 | async-start | bytes 3145728 | tf_op jit(solution)/shard_map/all_to_all | solution.py:135
  143.1 37.0 %collective-permute-start.13 = (bf16[384,384]{1,0:T(8,128)(2,1)}, bf16[384,384]{1,0:T(8,128)(2,1)}, u32[]{:S(2)}, u32[]{:S(2)}) collective-permute-start(bf16[384,384]{1,0:T(8,128)(2,1)} %get-tuple-element.47), channel_id=1, source_target_pairs={{0,12},{4,0},{8,4},{12,8},{1,13},{5,1},{9,5},{13,9},{2,14},{6,2},{... | collective-permute-start | bytes 884744 | tf_op jit(solution)/shard_map/ppermute | solution.py:154
  163.0 59.3 %collective-permute-start.6 = (bf16[768,384]{1,0:T(8,128)(2,1)}, bf16[768,384]{1,0:T(8,128)(2,1)}, u32[]{:S(2)}, u32[]{:S(2)}) collective-permute-start(bf16[768,384]{1,0:T(8,128)(2,1)} %fusion.2), channel_id=1, source_target_pairs={{0,4},{4,8},{8,12},{12,0},{1,5},{5,9},{9,13},{13,1},{2,6},{6,10},{... | collective-permute-start | bytes 1769480 | tf_op jit(solution)/shard_map/ppermute | solution.py:150
  172.5 25.9 %all-to-all-start.4 = ((bf16[4,384,128]{2,1,0:T(8,128)(2,1)}), bf16[4,384,128]{2,1,0:T(8,128)(2,1)}, u32[]{:S(2)}, u32[]{:S(2)}) async-start(bf16[4,384,128]{2,1,0:T(8,128)(2,1)} %copy.71), calls=%async_computation.4 | async-start | bytes 786432 | tf_op jit(solution)/shard_map/all_to_all | solution.py:195
  180.1 19.3 %copy-start.4 = (f32[4,384,128]{2,1,0:T(8,128)S(1)}, f32[4,384,128]{2,1,0:T(8,128)}, u32[]{:S(2)}) copy-start(f32[4,384,128]{2,1,0:T(8,128)} %copy-done.3) | copy-start | bytes 2359300
  180.1 24.1 %collective-permute-start.14 = (bf16[384,384]{1,0:T(8,128)(2,1)}, bf16[384,384]{1,0:T(8,128)(2,1)}, u32[]{:S(2)}, u32[]{:S(2)}) collective-permute-start(bf16[384,384]{1,0:T(8,128)(2,1)} %collective-permute-done.13), channel_id=1, source_target_pairs={{0,12},{4,0},{8,4},{12,8},{1,13},{5,1},{9,5},{13,9},{2,14},{6,2},{... | collective-permute-start | bytes 884744 | tf_op jit(solution)/shard_map/ppermute | solution.py:154
  200.7 28.6 %all-to-all-start.5 = ((bf16[4,384,128]{2,1,0:T(8,128)(2,1)}), bf16[4,384,128]{2,1,0:T(8,128)(2,1)S(1)}, u32[]{:S(2)}, u32[]{:S(2)}) async-start(bf16[4,384,128]{2,1,0:T(8,128)(2,1)} %get-tuple-element.45), calls=%async_computation.5 | async-start | bytes 786432 | tf_op jit(solution)/shard_map/all_to_all | solution.py:198
  218.6 12.5 %collective-permute-start.15 = (bf16[384,384]{1,0:T(8,128)(2,1)}, bf16[384,384]{1,0:T(8,128)(2,1)}, u32[]{:S(2)}, u32[]{:S(2)}) collective-permute-start(bf16[384,384]{1,0:T(8,128)(2,1)} %collective-permute-done.14), channel_id=1, source_target_pairs={{0,12},{4,0},{8,4},{12,8},{1,13},{5,1},{9,5},{13,9},{2,14},{6,2},{... | collective-permute-start | bytes 884744 | tf_op jit(solution)/shard_map/ppermute | solution.py:154
  222.3 5.1 %collective-permute-start.2 = (bf16[4,4,128]{2,1,0:T(4,128)(2,1)S(1)}, bf16[4,4,128]{2,1,0:T(4,128)(2,1)S(1)}, u32[]{:S(2)}, u32[]{:S(2)}) collective-permute-start(bf16[4,4,128]{2,1,0:T(4,128)(2,1)S(1)} %get-tuple-element.44), channel_id=1, source_target_pairs={{0,1},{1,0},{2,3},{3,2},{4,5},{5,4},{6,7},{7,6},{8,9},{9,8},{10,11... | collective-permute-start | bytes 12296 | tf_op jit(solution)/shard_map/ppermute | solution.py:165
  227.4 18.1 %collective-permute-start.7 = (bf16[768,384]{1,0:T(8,128)(2,1)}, bf16[768,384]{1,0:T(8,128)(2,1)}, u32[]{:S(2)}, u32[]{:S(2)}) collective-permute-start(bf16[768,384]{1,0:T(8,128)(2,1)} %get-tuple-element.49), channel_id=1, source_target_pairs={{0,4},{4,8},{8,12},{12,0},{1,5},{5,9},{9,13},{13,1},{2,6},{6,10},{... | collective-permute-start | bytes 1769480 | tf_op jit(solution)/shard_map/ppermute | solution.py:154
  227.4 18.1 %collective-permute-start.3 = (bf16[4,4,128]{2,1,0:T(4,128)(2,1)S(1)}, bf16[4,4,128]{2,1,0:T(4,128)(2,1)S(1)}, u32[]{:S(2)}, u32[]{:S(2)}) collective-permute-start(bf16[4,4,128]{2,1,0:T(4,128)(2,1)S(1)} %add_convert_fusion.1), channel_id=1, source_target_pairs={{0,2},{2,0},{1,3},{3,1},{4,6},{6,4},{5,7},{7,5},{8,10},{10,8},{9,1... | collective-permute-start | bytes 12296 | tf_op jit(solution)/shard_map/ppermute | solution.py:165
  230.8 17.5 %collective-permute-start = (bf16[512,512]{1,0:T(8,128)(2,1)}, bf16[512,512]{1,0:T(8,128)(2,1)}, u32[]{:S(2)}, u32[]{:S(2)}) collective-permute-start(bf16[512,512]{1,0:T(8,128)(2,1)} %convolution_convert_fusion), channel_id=1, source_target_pairs={{0,1},{1,0},{2,3},{3,2},{4,5},{5,4},{6,7},{7,6},{8,9},{9,8},{10,11... | collective-permute-start | bytes 1572872 | tf_op jit(solution)/shard_map/ppermute | solution.py:165
  232.7 30.6 %copy-start.9 = (bf16[384,4,128]{0,2,1:T(8,128)(2,1)S(1)}, bf16[384,4,128]{0,2,1:T(8,128)(2,1)}, u32[]{:S(2)}) copy-start(bf16[384,4,128]{0,2,1:T(8,128)(2,1)} %copy-done.8) | copy-start | bytes 1179652
  245.5 17.8 %copy-start.10 = (f32[384,512]{1,0:T(8,128)S(1)}, f32[384,512]{1,0:T(8,128)}, u32[]{:S(2)}) copy-start(f32[384,512]{1,0:T(8,128)} %bitcast_add_fusion) | copy-start | bytes 2359300
  245.5 17.8 %collective-permute-start.8 = (bf16[768,384]{1,0:T(8,128)(2,1)}, bf16[768,384]{1,0:T(8,128)(2,1)S(1)}, u32[]{:S(2)}, u32[]{:S(2)}) collective-permute-start(bf16[768,384]{1,0:T(8,128)(2,1)} %collective-permute-done.7), channel_id=1, source_target_pairs={{0,4},{4,8},{8,12},{12,0},{1,5},{5,9},{9,13},{13,1},{2,6},{6,10},{... | collective-permute-start | bytes 1769480 | tf_op jit(solution)/shard_map/ppermute | solution.py:154
  249.6 17.1 %collective-permute-start.1 = (bf16[512,512]{1,0:T(8,128)(2,1)S(1)}, bf16[512,512]{1,0:T(8,128)(2,1)S(1)}, u32[]{:S(2)}, u32[]{:S(2)}) collective-permute-start(bf16[512,512]{1,0:T(8,128)(2,1)S(1)} %add_convert_fusion), channel_id=1, source_target_pairs={{0,2},{2,0},{1,3},{3,1},{4,6},{6,4},{5,7},{7,5},{8,10},{10,8},{9,1... | collective-permute-start | bytes 1572872 | tf_op jit(solution)/shard_map/ppermute | solution.py:165
  263.3 16.8 %collective-permute-start.9 = (bf16[768,384]{1,0:T(8,128)(2,1)S(1)}, bf16[768,384]{1,0:T(8,128)(2,1)S(1)}, u32[]{:S(2)}, u32[]{:S(2)}) collective-permute-start(bf16[768,384]{1,0:T(8,128)(2,1)S(1)} %collective-permute-done.8), channel_id=1, source_target_pairs={{0,4},{4,8},{8,12},{12,0},{1,5},{5,9},{9,13},{13,1},{2,6},{6,10},{... | collective-permute-start | bytes 1769480 | tf_op jit(solution)/shard_map/ppermute | solution.py:154
  (7 other events, 17.9 us)
Sparse Core Ops, SparseCore 0:
  11.5 22.3 all-gather.4
  48.3 18.7 all-gather.2

commit v2 on v1

--- a/solution.py
+++ b/solution.py
@@ -55,7 +55,10 @@
         slope = half + (0.5 * root) * s0 * (1.0 - t * t) * (1.0 + 3 * 0.044715 * square)
         hidden = (gelu * s1).astype(BF16)
         reduced_acc[j] += dot(down_ref[j], hidden, ((0,), (0,)))
-        down_grad_ref[j] = dot(cot_all[j], hidden, ((1,), (1,))).astype(BF16)
+        down_grad = dot(cot_all[j], hidden, ((1,), (1,)))
+        chunk = down_grad_ref.shape[2]
+        for d in range(down_grad_ref.shape[0]):
+            down_grad_ref[d, j] = down_grad[d * chunk:(d + 1) * chunk].astype(BF16)
         hidden_cot = dot(down_ref[j], cot_all[j], ((1,), (0,)))
         cots[0].append(hidden_cot * s1 * slope)
         cots[1].append(hidden_cot * gelu)
@@ -82,6 +85,8 @@
     if part % 16:
         x = jnp.swapaxes(x, 0, 1).reshape(1, blocks, chans, tokens)
         cot = jnp.swapaxes(cot, 0, 1).reshape(1, blocks, chans, tokens)
+    n = lax.axis_size("seq")
+    chunks = n if (chans // n) % 16 == 0 else 1
     tile = 128 if hidden % 128 == 0 else hidden
     down = jnp.transpose(down_first, (1, 2, 0))
     mix = jnp.transpose(up_second, (1, 0, 2, 3)).reshape(hidden, 2 * blocks * blocks).astype(F32)
@@ -102,13 +107,13 @@
             whole,
             whole,
             pl.BlockSpec((2, blocks, tile, chans), lambda i: (0, 0, i, 0)),
-            pl.BlockSpec((blocks, chans, tile), lambda i: (0, 0, i)),
+            pl.BlockSpec((chunks, blocks, chans // chunks, tile), lambda i: (0, 0, 0, i)),
         ],
         out_shape=[
             jax.ShapeDtypeStruct(x.shape, BF16),
             jax.ShapeDtypeStruct(x.shape, BF16),
             jax.ShapeDtypeStruct((2, blocks, hidden, chans), BF16),
-            jax.ShapeDtypeStruct((blocks, chans, hidden), BF16),
+            jax.ShapeDtypeStruct((chunks, blocks, chans // chunks, hidden), BF16),
         ],
         scratch_shapes=[
             pltpu.VMEM((blocks, chans, tokens), BF16),
@@ -128,6 +133,8 @@
     if part % 16:
         back = jnp.swapaxes(back.reshape(blocks, shares, part, tokens), 0, 1)
         reduced = jnp.swapaxes(reduced.reshape(blocks, shares, part, tokens), 0, 1)
+    if chunks != n:
+        down_grad = jnp.swapaxes(down_grad.reshape(blocks, n, chans // n, hidden), 0, 1)
     return back, reduced, up_grad, down_grad
 
 
@@ -136,24 +143,26 @@
     return jnp.sum(moved.astype(F32), axis=0)
 
 
-def ring_sum(x, axis, way):
+def ring_sums(parts, axis):
     n = lax.axis_size(axis)
     me = lax.axis_index(axis)
-    perm = [(i, (i + way) % n) for i in range(n)]
-    rows = x.reshape(n, -1, x.shape[-1])
-
-    def own(back):
+    perms = {way: [(i, (i + way) % n) for i in range(n)] for way in (1, -1)}
+
+    def own(rows, way, back):
         return lax.dynamic_index_in_dim(rows, (me - way * back) % n, 0, keepdims=False)
 
-    held = own(1)
+    held = [own(rows, way, 1) for rows, way in parts]
     for s in range(n - 1):
-        held = (lax.ppermute(held, axis, perm).astype(F32) + own(s + 2).astype(F32)).astype(BF16)
-    out = jnp.zeros(rows.shape, F32)
-    out = lax.dynamic_update_index_in_dim(out, held.astype(F32), me, 0)
+        held = [
+            (lax.ppermute(h, axis, perms[way]).astype(F32) + own(rows, way, s + 2).astype(F32)).astype(BF16)
+            for h, (rows, way) in zip(held, parts)
+        ]
+    pieces = [[(me, h)] for h in held]
     for s in range(n - 1):
-        held = lax.ppermute(held, axis, perm)
-        out = lax.dynamic_update_index_in_dim(out, held.astype(F32), (me - way * (s + 1)) % n, 0)
-    return out.reshape(x.shape)
+        held = [lax.ppermute(h, axis, perms[way]) for h, (_, way) in zip(held, parts)]
+        for got, h, (_, way) in zip(pieces, held, parts):
+            got.append(((me - way * (s + 1)) % n, h))
+    return pieces
 
 
 def swap_sum(x):
@@ -220,8 +229,23 @@
     back, reduced, up_grad, down_grad = channel_block(
         x_all, cot_all, up_first, up_second, up_shift, down_first
     )
-    up_first_grad = ring_sum(up_grad, "seq", 1)
-    down_first_grad = jnp.swapaxes(ring_sum(down_grad, "seq", -1), 0, 1)
+    up_rows = up_grad.reshape(2, n, -1, up_grad.shape[-1])
+    gate_pieces, value_pieces, down_pieces = ring_sums(
+        [(up_rows[0], 1), (up_rows[1], -1), (down_grad, 1)], "seq"
+    )
+    up_first_grad = jnp.zeros(up_rows.shape, F32)
+    for s in range(n):
+        for g, pieces in enumerate((gate_pieces, value_pieces)):
+            at, piece = pieces[s]
+            up_first_grad = lax.dynamic_update_slice(
+                up_first_grad, piece.astype(F32)[None, None], (g, at, 0, 0)
+            )
+    up_first_grad = up_first_grad.reshape(up_grad.shape)
+    share = down_grad.shape[2]
+    down_first_grad = jnp.zeros((n * share,) + (blocks, down_grad.shape[3]), F32)
+    for at, piece in down_pieces:
+        turned = lax.optimization_barrier(jnp.swapaxes(piece, 0, 1).astype(F32))
+        down_first_grad = lax.dynamic_update_slice(down_first_grad, turned, (at * share, 0, 0))
 
     input_cot = pieces_sum(back, PLANE).reshape(rows, length)
     total_cot = cotangent.reshape(rows, length).astype(F32) + input_cot

time: 291 us -> 270 us (0.928)
  local copies, waits for them, and re-layouts: 70.6 us -> 25.6 us
  starting transfers between devices: 48.9 us -> 64.9 us
  waiting for transfers between devices: 77.9 us -> 88.7 us
    dynamic_update_slice x4, local copies, waits for them, and re-layouts: 51.1 us -> 4.79 us  [per_device(): lax.dynamic_update_slice(down_first_grad, turned, (at * share, 0, 0))]
    all_to_all x1, starting transfers between devices: 3.46 us -> 16.3 us  [to_blocks(): x = lax.all_to_all(x, 'seq', split_axis=0, concat_axis=0, tiled=True)]
    ppermute x4, waiting for transfers between devices: 0.01 us -> 9.45 us  [swap_sum(): got = lax.ppermute(sent, axis, [(i, i ^ bit) for i in range(n)])]
    ppermute x12 -> x18, waiting for transfers between devices: 50.2 us -> 41.2 us  [the longest x9 29.4 us: ring_sums(): lax.ppermute(h, axis, perms[way]).astype(F32)]
    all_to_all x2, waiting for transfers between devices: 0.01 us -> 8.03 us  [pieces_sum(): moved = lax.all_to_all(x, axes, split_axis=0, concat_axis=0, tiled=True)]
    dynamic_update_slice x4 -> x8, other arithmetic: 6.92 us -> 14.9 us  [per_device(): lax.dynamic_update_slice(up_first_grad, piece.astype(F32)[None, None], (g...]
    ppermute x12 -> x18, starting transfers between devices: 21.4 us -> 26.8 us  [the longest x9 15.4 us: ring_sums(): lax.ppermute(h, axis, perms[way])]
    all_to_all x1, waiting for transfers between devices: 0.01 us -> 4.85 us  [to_blocks(): x = lax.all_to_all(x, 'seq', split_axis=0, concat_axis=0, tiled=True)]
  transfers between devices with their start and end apart: 23 -> 29, of which waited for: 7 -> 16; matrix products, arithmetic and copies ran while one was open for 37% -> 22% of each run, Pallas kernels for 0% -> 0%
where the time goes in v2:
time: 270 us; the launch traced here: 269 us
  waiting for transfers between devices  88.7 us (33%)
  starting transfers between devices  64.9 us (24%)
  other arithmetic  41.9 us (16%)
  local copies, waits for them, and re-layouts  25.6 us (9%)
  Pallas kernels  18.5 us (7%)
  between operations  14.5 us (5%)
  blocking collectives  13.3 us (5%)
    ppermute x9, waiting for transfers between devices, ring_sums(): lax.ppermute(h, axis, perms[way]).astype(F32)  29.4 us
    pallas_call x1, Pallas kernels, channel_block(): pl.pallas_call(channel_kernel, grid=(hidden // tile,), in_specs=[whole, w...  18.5 us
    all_to_all x1, starting transfers between devices, to_blocks(): x = lax.all_to_all(x, 'seq', split_axis=0, concat_axis=0, tiled=True)  16.3 us
    ppermute x9, starting transfers between devices, ring_sums(): lax.ppermute(h, axis, perms[way])  15.4 us
    dynamic_update_slice x8, other arithmetic, per_device(): lax.dynamic_update_slice(up_first_grad, piece.astype(F32)[None, None], (g...  14.9 us
    all_gather x1, waiting for transfers between devices, per_device(): x_all = lax.all_gather(block_in, PLANE, axis=0)  13.4 us
    all_to_all x1, blocking collectives, to_blocks(): x = lax.all_to_all(x, 'seq', split_axis=0, concat_axis=0, tiled=True)  13.3 us
    ppermute x9, waiting for transfers between devices, ring_sums(): lax.ppermute(h, axis, perms[way])  11.8 us
  transfers between devices with their start and end apart: 29, of which 16 were waited for; matrix products, arithmetic and copies ran while one was open for 22% of the time, Pallas kernels for 0%

profile of v2, /device:TPU:0, one launch (start us, length us, event | category | flops | bytes accessed | tf_op | source)
XLA Modules:
  0.0 268.8 jit_solution(8278426455373930071)
XLA Ops:
  12.6 6.3 %all-to-all-start = ((bf16[4,384,128]{2,1,0:T(8,128)(2,1)}), bf16[4,384,128]{2,1,0:T(8,128)(2,1)S(1)}, u32[]{:S(2)}, u32[]{:S(2)}) async-start(bf16[4,384,128]{2,1,0:T(8,128)(2,1)} %bitcast.259), calls=%async_computation | async-start | bytes 786432 | tf_op jit(solution)/shard_map/all_to_all | solution.py:204
  19.0 11.7 %all-to-all-done = bf16[4,384,128]{2,1,0:T(8,128)(2,1)S(1)} async-done(((bf16[4,384,128]{2,1,0:T(8,128)(2,1)}), bf16[4,384,128]{2,1,0:T(8,128)(2,1)S(1)}, u32[]{:S(2)}, u32[]{:S(2)}) %all-to-all-start) | async-done | bytes 393248 | tf_op jit(solution)/shard_map/all_to_all | solution.py:204
  31.8 13.3 %all_to_all.30 = bf16[4,384,128]{2,1,0:T(8,128)(2,1)S(1)} all-to-all(bf16[4,384,128]{2,1,0:T(8,128)(2,1)S(1)} %multiply_reduce_fusion.2), channel_id=1, replica_groups=mesh['grp'=2,'seq'=4,'ch'=2,'sub'=2] {'seq'}, dimensions={0} | all-to-all | bytes 786432 | tf_op jit(solution)/shard_map/all_to_all | solution.py:207
  49.5 2.5 copy.68
  53.6 13.4 %all-gather.3.cloned.1.call-done.x_ref = bf16[4,4,96,512]{3,2,1,0:T(8,128)(2,1)} async-done(((bf16[1,4,96,512]{3,2,1,0:T(8,128)(2,1)}), bf16[4,4,96,512]{3,2,1,0:T(8,128)(2,1)}) %all-gather.3.cloned.1.call-update) | async-done | bytes 1572880 | tf_op jit(solution)/shard_map/all_gather | solution.py:228
  67.0 18.5 %shard_map.154 = (bf16[4,4,96,512]{3,2,1,0:T(8,128)(2,1)}, bf16[4,4,96,512]{3,2,1,0:T(8,128)(2,1)}, bf16[2,4,384,384]{3,2,1,0:T(8,128)(2,1)}, bf16[4,4,96,384]{3,2,1,0:T(8,128)(2,1)S(1)}) custom-call(bf16[4,4,96,512]{3,2,1,0:T(8,128)(2,1)} %all-gather.3.cloned.1.call-done.x_ref, bf16[4,4,96,512]{3,2,1,0:T(8,128)(2,1)} %all-gather.5.cloned.1.call-done.cot_ref, ...), custom_call_target="tpu_custom_call" | custom-call | flops 5435817984 | bytes 14680064 | tf_op jit(solution)/shard_map/pallas_call | solution.py:95
  85.5 3.0 %fusion.62 = (bf16[1,4,384,384]{3,2,1,0:T(8,128)(2,1)S(1)}, bf16[1,4,384,384]{3,2,1,0:T(8,128)(2,1)}) fusion(bf16[2,4,384,384]{3,2,1,0:T(8,128)(2,1)} %get-tuple-element.12), kind=kLoop, calls=%fused_computation.155 | loop fusion | bytes 4718592 | tf_op jit(solution)/shard_map/slice | solution.py:234
  92.8 4.3 %all-to-all-start.2 = ((bf16[4,4,96,512]{3,2,1,0:T(8,128)(2,1)}), bf16[4,4,96,512]{3,2,1,0:T(8,128)(2,1)}, u32[]{:S(2)}, u32[]{:S(2)}) async-start(bf16[4,4,96,512]{3,2,1,0:T(8,128)(2,1)} %get-tuple-element.10), calls=%async_computation.2 | async-start | bytes 3145728 | tf_op jit(solution)/shard_map/all_to_all | solution.py:142
  97.2 2.4 collective-permute-start.7
  102.8 4.9 %collective-permute-done.7 = bf16[384,384]{1,0:T(8,128)(2,1)S(1)} collective-permute-done((bf16[384,384]{1,0:T(8,128)(2,1)S(1)}, bf16[384,384]{1,0:T(8,128)(2,1)S(1)}, u32[]{:S(2)}, u32[]{:S(2)}) %collective-permute-start.7) | collective-permute-done | bytes 294944 | tf_op jit(solution)/shard_map/ppermute | solution.py:157
  107.8 3.6 %collective-permute-start.8 = (bf16[384,384]{1,0:T(8,128)(2,1)S(1)}, bf16[384,384]{1,0:T(8,128)(2,1)S(1)}, u32[]{:S(2)}, u32[]{:S(2)}) collective-permute-start(bf16[384,384]{1,0:T(8,128)(2,1)S(1)} %fusion.24), channel_id=1, source_target_pairs={{0,12},{4,0},{8,4},{12,8},{1,13},{5,1},{9,5},{13,9},{2,14},{6,2},{... | collective-permute-start | bytes 884744 | tf_op jit(solution)/shard_map/ppermute | solution.py:157
  111.4 4.0 %collective-permute-done.16 = bf16[4,96,384]{2,1,0:T(8,128)(2,1)S(1)} collective-permute-done((bf16[4,96,384]{2,1,0:T(8,128)(2,1)S(1)}, bf16[4,96,384]{2,1,0:T(8,128)(2,1)S(1)}, u32[]{:S(2)}, u32[]{:S(2)}) %collective-permute-start.16) | collective-permute-done | bytes 294944 | tf_op jit(solution)/shard_map/ppermute | solution.py:157
  115.9 5.7 %collective-permute-done.5 = bf16[384,384]{1,0:T(8,128)(2,1)S(1)} collective-permute-done((bf16[384,384]{1,0:T(8,128)(2,1)S(1)}, bf16[384,384]{1,0:T(8,128)(2,1)S(1)}, u32[]{:S(2)}, u32[]{:S(2)}) %collective-permute-start.5) | collective-permute-done | bytes 294944 | tf_op jit(solution)/shard_map/ppermute | solution.py:157
  123.2 4.7 %collective-permute-done.8 = bf16[384,384]{1,0:T(8,128)(2,1)S(1)} collective-permute-done((bf16[384,384]{1,0:T(8,128)(2,1)S(1)}, bf16[384,384]{1,0:T(8,128)(2,1)S(1)}, u32[]{:S(2)}, u32[]{:S(2)}) %collective-permute-start.8) | collective-permute-done | bytes 294944 | tf_op jit(solution)/shard_map/ppermute | solution.py:157
  128.7 2.4 collective-permute-start.9
  131.1 3.3 %collective-permute-done.17 = bf16[4,96,384]{2,1,0:T(8,128)(2,1)S(1)} collective-permute-done((bf16[4,96,384]{2,1,0:T(8,128)(2,1)S(1)}, bf16[4,96,384]{2,1,0:T(8,128)(2,1)S(1)}, u32[]{:S(2)}, u32[]{:S(2)}) %collective-permute-start.17) | collective-permute-done | bytes 294944 | tf_op jit(solution)/shard_map/ppermute | solution.py:157
  135.6 5.0 %collective-permute-done.6 = bf16[384,384]{1,0:T(8,128)(2,1)S(1)} collective-permute-done((bf16[384,384]{1,0:T(8,128)(2,1)S(1)}, bf16[384,384]{1,0:T(8,128)(2,1)S(1)}, u32[]{:S(2)}, u32[]{:S(2)}) %collective-permute-start.6) | collective-permute-done | bytes 294944 | tf_op jit(solution)/shard_map/ppermute | solution.py:157
  140.6 2.6 broadcast_in_dim.64
  145.6 4.4 %all-to-all-start.3 = ((bf16[4,4,96,512]{3,2,1,0:T(8,128)(2,1)}), bf16[4,4,96,512]{3,2,1,0:T(8,128)(2,1)}, u32[]{:S(2)}, u32[]{:S(2)}) async-start(bf16[4,4,96,512]{3,2,1,0:T(8,128)(2,1)} %get-tuple-element.11), calls=%async_computation.3 | async-start | bytes 3145728 | tf_op jit(solution)/shard_map/all_to_all | solution.py:142
  150.0 1.9 convert_dynamic-update-slice_fusion.6
  152.0 3.3 %collective-permute-start.11 = (bf16[384,384]{1,0:T(8,128)(2,1)}, bf16[384,384]{1,0:T(8,128)(2,1)}, u32[]{:S(2)}, u32[]{:S(2)}) collective-permute-start(bf16[384,384]{1,0:T(8,128)(2,1)} %get-tuple-element.49), channel_id=1, source_target_pairs={{0,12},{4,0},{8,4},{12,8},{1,13},{5,1},{9,5},{13,9},{2,14},{6,2},{... | collective-permute-start | bytes 884744 | tf_op jit(solution)/shard_map/ppermute | solution.py:162
  162.1 8.0 %all-to-all-done.3 = bf16[4,4,96,512]{3,2,1,0:T(8,128)(2,1)} async-done(((bf16[4,4,96,512]{3,2,1,0:T(8,128)(2,1)}), bf16[4,4,96,512]{3,2,1,0:T(8,128)(2,1)}, u32[]{:S(2)}, u32[]{:S(2)}) %all-to-all-start.3) | async-done | bytes 1572896 | tf_op jit(solution)/shard_map/all_to_all | solution.py:142
  173.0 2.7 %fusion.30 = bf16[4,384,128]{2,0,1:T(4,128)(2,1)S(1)} fusion(f32[384]{0:T(512)S(1)} %add.458, f32[384,4,128]{2,1,0:T(4,128)} %reshape.1255, f32[384]{0:T(512)S(1)} %mul.582, f32[384,4,128]{2,1,0:T(4,128)S(1)} %copy-done.9, f32[384,4,128]{2,1,0:T(4,128)} %reshape.1238), kind=kLoop, calls=%fused_computation.79 | loop fusion | flops 1572864 | bytes 2755584 | tf_op jit(solution)/shard_map/transpose | solution.py:203
  176.5 4.6 %all-to-all-start.4 = ((bf16[4,384,128]{2,1,0:T(8,128)(2,1)}), bf16[4,384,128]{2,1,0:T(8,128)(2,1)S(1)}, u32[]{:S(2)}, u32[]{:S(2)}) async-start(bf16[4,384,128]{2,1,0:T(8,128)(2,1)} %copy.71), calls=%async_computation.4 | async-start | bytes 786432 | tf_op jit(solution)/shard_map/all_to_all | solution.py:204
  184.3 2.0 collective-permute-start.20
  189.6 2.4 collective-permute-start.13
  193.8 5.8 %collective-permute-done.20 = bf16[4,96,384]{2,1,0:T(8,128)(2,1)} collective-permute-done((bf16[4,96,384]{2,1,0:T(8,128)(2,1)}, bf16[4,96,384]{2,1,0:T(8,128)(2,1)}, u32[]{:S(2)}, u32[]{:S(2)}) %collective-permute-start.20) | collective-permute-done | bytes 294944 | tf_op jit(solution)/shard_map/ppermute | solution.py:162
  200.7 5.2 %collective-permute-done.12 = bf16[384,384]{1,0:T(8,128)(2,1)} collective-permute-done((bf16[384,384]{1,0:T(8,128)(2,1)}, bf16[384,384]{1,0:T(8,128)(2,1)}, u32[]{:S(2)}, u32[]{:S(2)}) %collective-permute-start.12) | collective-permute-done | bytes 294944 | tf_op jit(solution)/shard_map/ppermute | solution.py:162
  205.9 5.5 %collective-permute-start.14 = (bf16[384,384]{1,0:T(8,128)(2,1)}, bf16[384,384]{1,0:T(8,128)(2,1)}, u32[]{:S(2)}, u32[]{:S(2)}) collective-permute-start(bf16[384,384]{1,0:T(8,128)(2,1)} %collective-permute-done.12), channel_id=1, source_target_pairs={{0,4},{4,8},{8,12},{12,0},{1,5},{5,9},{9,13},{13,1},{2,6},{6,10},{... | collective-permute-start | bytes 884744 | tf_op jit(solution)/shard_map/ppermute | solution.py:162
  216.6 16.3 %all-to-all-start.5 = ((bf16[4,384,128]{2,1,0:T(8,128)(2,1)}), bf16[4,384,128]{2,1,0:T(8,128)(2,1)S(1)}, u32[]{:S(2)}, u32[]{:S(2)}) async-start(bf16[4,384,128]{2,1,0:T(8,128)(2,1)} %get-tuple-element.45), calls=%async_computation.5 | async-start | bytes 786432 | tf_op jit(solution)/shard_map/all_to_all | solution.py:207
  236.9 4.9 %all-to-all-done.5 = bf16[4,384,128]{2,1,0:T(8,128)(2,1)S(1)} async-done(((bf16[4,384,128]{2,1,0:T(8,128)(2,1)}), bf16[4,384,128]{2,1,0:T(8,128)(2,1)S(1)}, u32[]{:S(2)}, u32[]{:S(2)}) %all-to-all-start.5) | async-done | bytes 393248 | tf_op jit(solution)/shard_map/all_to_all | solution.py:207
  252.8 8.0 %collective-permute-done.1 = bf16[512,512]{1,0:T(8,128)(2,1)S(1)} collective-permute-done((bf16[512,512]{1,0:T(8,128)(2,1)S(1)}, bf16[512,512]{1,0:T(8,128)(2,1)S(1)}, u32[]{:S(2)}, u32[]{:S(2)}) %collective-permute-start.1) | collective-permute-done | bytes 524320 | tf_op jit(solution)/shard_map/ppermute | solution.py:174
  (135 shorter events, 67.7 us)
Async XLA Ops:
  7.2 46.4 %all-gather.5.cloned.1.call-start = ((), (), s32[]{:S(2)}) async-start(), calls=%async_computation.7 | async-start | bytes 1966080 | tf_op jit(solution)/shard_map/all_gather | solution.py:219
  9.3 9.7 %copy-start.15 = (bf16[128,4,4]{0,2,1:T(4,128)(2,1)S(1)}, bf16[128,4,4]{0,2,1:T(4,128)(2,1)}, u32[]{:S(2)}) copy-start(bf16[128,4,4]{0,2,1:T(4,128)(2,1)} %param.15) | copy-start | bytes 12292
  12.6 18.0 %all-to-all-start = ((bf16[4,384,128]{2,1,0:T(8,128)(2,1)}), bf16[4,384,128]{2,1,0:T(8,128)(2,1)S(1)}, u32[]{:S(2)}, u32[]{:S(2)}) async-start(bf16[4,384,128]{2,1,0:T(8,128)(2,1)} %bitcast.259), calls=%async_computation | async-start | bytes 786432 | tf_op jit(solution)/shard_map/all_to_all | solution.py:204
  18.9 48.1 %all-gather.3.cloned.1.call-start = ((), (), s32[]{:S(2)}) async-start(), calls=%async_computation.6 | async-start | bytes 1966080 | tf_op jit(solution)/shard_map/all_gather | solution.py:228
  90.2 11.4 %collective-permute-start.4 = (bf16[384,384]{1,0:T(8,128)(2,1)}, bf16[384,384]{1,0:T(8,128)(2,1)}, u32[]{:S(2)}, u32[]{:S(2)}) collective-permute-start(bf16[384,384]{1,0:T(8,128)(2,1)} %dynamic-slice_bitcast_fusion.2), channel_id=1, source_target_pairs={{0,4},{4,8},{8,12},{12,0},{1,5},{5,9},{9,13},{13,1},{2,6},{6,10},{... | collective-permute-start | bytes 884744 | tf_op jit(solution)/shard_map/ppermute | solution.py:157
  92.8 52.8 %all-to-all-start.2 = ((bf16[4,4,96,512]{3,2,1,0:T(8,128)(2,1)}), bf16[4,4,96,512]{3,2,1,0:T(8,128)(2,1)}, u32[]{:S(2)}, u32[]{:S(2)}) async-start(bf16[4,4,96,512]{3,2,1,0:T(8,128)(2,1)} %get-tuple-element.10), calls=%async_computation.2 | async-start | bytes 3145728 | tf_op jit(solution)/shard_map/all_to_all | solution.py:142
  97.2 10.5 %collective-permute-start.7 = (bf16[384,384]{1,0:T(8,128)(2,1)S(1)}, bf16[384,384]{1,0:T(8,128)(2,1)S(1)}, u32[]{:S(2)}, u32[]{:S(2)}) collective-permute-start(bf16[384,384]{1,0:T(8,128)(2,1)S(1)} %dynamic-slice_bitcast_fusion.1), channel_id=1, source_target_pairs={{0,12},{4,0},{8,4},{12,8},{1,13},{5,1},{9,5},{13,9},{2,14},{6,2},{... | collective-permute-start | bytes 884744 | tf_op jit(solution)/shard_map/ppermute | solution.py:157
  99.7 15.8 %collective-permute-start.16 = (bf16[4,96,384]{2,1,0:T(8,128)(2,1)S(1)}, bf16[4,96,384]{2,1,0:T(8,128)(2,1)S(1)}, u32[]{:S(2)}, u32[]{:S(2)}) collective-permute-start(bf16[4,96,384]{2,1,0:T(8,128)(2,1)S(1)} %dynamic-slice_bitcast_fusion), channel_id=1, source_target_pairs={{0,4},{4,8},{8,12},{12,0},{1,5},{5,9},{9,13},{13,1},{2,6},{6,10},{... | collective-permute-start | bytes 884744 | tf_op jit(solution)/shard_map/ppermute | solution.py:157
  102.7 18.9 %collective-permute-start.5 = (bf16[384,384]{1,0:T(8,128)(2,1)S(1)}, bf16[384,384]{1,0:T(8,128)(2,1)S(1)}, u32[]{:S(2)}, u32[]{:S(2)}) collective-permute-start(bf16[384,384]{1,0:T(8,128)(2,1)S(1)} %fusion.27), channel_id=1, source_target_pairs={{0,4},{4,8},{8,12},{12,0},{1,5},{5,9},{9,13},{13,1},{2,6},{6,10},{... | collective-permute-start | bytes 884744 | tf_op jit(solution)/shard_map/ppermute | solution.py:157
  107.8 20.1 %collective-permute-start.8 = (bf16[384,384]{1,0:T(8,128)(2,1)S(1)}, bf16[384,384]{1,0:T(8,128)(2,1)S(1)}, u32[]{:S(2)}, u32[]{:S(2)}) collective-permute-start(bf16[384,384]{1,0:T(8,128)(2,1)S(1)} %fusion.24), channel_id=1, source_target_pairs={{0,12},{4,0},{8,4},{12,8},{1,13},{5,1},{9,5},{13,9},{2,14},{6,2},{... | collective-permute-start | bytes 884744 | tf_op jit(solution)/shard_map/ppermute | solution.py:157
  115.5 18.9 %collective-permute-start.17 = (bf16[4,96,384]{2,1,0:T(8,128)(2,1)S(1)}, bf16[4,96,384]{2,1,0:T(8,128)(2,1)S(1)}, u32[]{:S(2)}, u32[]{:S(2)}) collective-permute-start(bf16[4,96,384]{2,1,0:T(8,128)(2,1)S(1)} %fusion.21), channel_id=1, source_target_pairs={{0,4},{4,8},{8,12},{12,0},{1,5},{5,9},{9,13},{13,1},{2,6},{6,10},{... | collective-permute-start | bytes 884744 | tf_op jit(solution)/shard_map/ppermute | solution.py:157
  122.7 18.0 %collective-permute-start.6 = (bf16[384,384]{1,0:T(8,128)(2,1)S(1)}, bf16[384,384]{1,0:T(8,128)(2,1)S(1)}, u32[]{:S(2)}, u32[]{:S(2)}) collective-permute-start(bf16[384,384]{1,0:T(8,128)(2,1)S(1)} %fusion.26), channel_id=1, source_target_pairs={{0,4},{4,8},{8,12},{12,0},{1,5},{5,9},{9,13},{13,1},{2,6},{6,10},{... | collective-permute-start | bytes 884744 | tf_op jit(solution)/shard_map/ppermute | solution.py:157
  128.7 21.3 %collective-permute-start.9 = (bf16[384,384]{1,0:T(8,128)(2,1)}, bf16[384,384]{1,0:T(8,128)(2,1)}, u32[]{:S(2)}, u32[]{:S(2)}) collective-permute-start(bf16[384,384]{1,0:T(8,128)(2,1)} %fusion.23), channel_id=1, source_target_pairs={{0,12},{4,0},{8,4},{12,8},{1,13},{5,1},{9,5},{13,9},{2,14},{6,2},{... | collective-permute-start | bytes 884744 | tf_op jit(solution)/shard_map/ppermute | solution.py:157
  135.2 20.1 %collective-permute-start.18 = (bf16[4,96,384]{2,1,0:T(8,128)(2,1)}, bf16[4,96,384]{2,1,0:T(8,128)(2,1)}, u32[]{:S(2)}, u32[]{:S(2)}) collective-permute-start(bf16[4,96,384]{2,1,0:T(8,128)(2,1)} %fusion.20), channel_id=1, source_target_pairs={{0,4},{4,8},{8,12},{12,0},{1,5},{5,9},{9,13},{13,1},{2,6},{6,10},{... | collective-permute-start | bytes 884744 | tf_op jit(solution)/shard_map/ppermute | solution.py:157
  145.1 41.1 %collective-permute-start.10 = (bf16[384,384]{1,0:T(8,128)(2,1)}, bf16[384,384]{1,0:T(8,128)(2,1)}, u32[]{:S(2)}, u32[]{:S(2)}) collective-permute-start(bf16[384,384]{1,0:T(8,128)(2,1)} %get-tuple-element.51), channel_id=1, source_target_pairs={{0,4},{4,8},{8,12},{12,0},{1,5},{5,9},{9,13},{13,1},{2,6},{6,10},{... | collective-permute-start | bytes 884744 | tf_op jit(solution)/shard_map/ppermute | solution.py:162
  145.6 24.5 %all-to-all-start.3 = ((bf16[4,4,96,512]{3,2,1,0:T(8,128)(2,1)}), bf16[4,4,96,512]{3,2,1,0:T(8,128)(2,1)}, u32[]{:S(2)}, u32[]{:S(2)}) async-start(bf16[4,4,96,512]{3,2,1,0:T(8,128)(2,1)} %get-tuple-element.11), calls=%async_computation.3 | async-start | bytes 3145728 | tf_op jit(solution)/shard_map/all_to_all | solution.py:142
  152.0 37.6 %collective-permute-start.11 = (bf16[384,384]{1,0:T(8,128)(2,1)}, bf16[384,384]{1,0:T(8,128)(2,1)}, u32[]{:S(2)}, u32[]{:S(2)}) collective-permute-start(bf16[384,384]{1,0:T(8,128)(2,1)} %get-tuple-element.49), channel_id=1, source_target_pairs={{0,12},{4,0},{8,4},{12,8},{1,13},{5,1},{9,5},{13,9},{2,14},{6,2},{... | collective-permute-start | bytes 884744 | tf_op jit(solution)/shard_map/ppermute | solution.py:162
  157.1 25.0 %collective-permute-start.19 = (bf16[4,96,384]{2,1,0:T(8,128)(2,1)}, bf16[4,96,384]{2,1,0:T(8,128)(2,1)}, u32[]{:S(2)}, u32[]{:S(2)}) collective-permute-start(bf16[4,96,384]{2,1,0:T(8,128)(2,1)} %get-tuple-element.47), channel_id=1, source_target_pairs={{0,4},{4,8},{8,12},{12,0},{1,5},{5,9},{9,13},{13,1},{2,6},{6,10},{... | collective-permute-start | bytes 884744 | tf_op jit(solution)/shard_map/ppermute | solution.py:162
  161.9 11.1 %copy-start.9 = (f32[384,4,128]{2,1,0:T(4,128)S(1)}, f32[384,4,128]{2,1,0:T(4,128)}, u32[]{:S(2)}) copy-start(f32[384,4,128]{2,1,0:T(4,128)} %reshape.1254) | copy-start | bytes 2359300
  176.5 38.8 %all-to-all-start.4 = ((bf16[4,384,128]{2,1,0:T(8,128)(2,1)}), bf16[4,384,128]{2,1,0:T(8,128)(2,1)S(1)}, u32[]{:S(2)}, u32[]{:S(2)}) async-start(bf16[4,384,128]{2,1,0:T(8,128)(2,1)} %copy.71), calls=%async_computation.4 | async-start | bytes 786432 | tf_op jit(solution)/shard_map/all_to_all | solution.py:204
  184.3 15.3 %collective-permute-start.20 = (bf16[4,96,384]{2,1,0:T(8,128)(2,1)}, bf16[4,96,384]{2,1,0:T(8,128)(2,1)}, u32[]{:S(2)}, u32[]{:S(2)}) collective-permute-start(bf16[4,96,384]{2,1,0:T(8,128)(2,1)} %collective-permute-done.19), channel_id=1, source_target_pairs={{0,4},{4,8},{8,12},{12,0},{1,5},{5,9},{9,13},{13,1},{2,6},{6,10},{... | collective-permute-start | bytes 884744 | tf_op jit(solution)/shard_map/ppermute | solution.py:162
  186.3 19.6 %collective-permute-start.12 = (bf16[384,384]{1,0:T(8,128)(2,1)}, bf16[384,384]{1,0:T(8,128)(2,1)}, u32[]{:S(2)}, u32[]{:S(2)}) collective-permute-start(bf16[384,384]{1,0:T(8,128)(2,1)} %collective-permute-done.10), channel_id=1, source_target_pairs={{0,4},{4,8},{8,12},{12,0},{1,5},{5,9},{9,13},{13,1},{2,6},{6,10},{... | collective-permute-start | bytes 884744 | tf_op jit(solution)/shard_map/ppermute | solution.py:162
  189.6 25.8 %copy-start.4 = (f32[4,384,128]{2,1,0:T(8,128)S(1)}, f32[4,384,128]{2,1,0:T(8,128)}, u32[]{:S(2)}) copy-start(f32[4,384,128]{2,1,0:T(8,128)} %copy-done.3) | copy-start | bytes 2359300
  189.6 22.6 %collective-permute-start.13 = (bf16[384,384]{1,0:T(8,128)(2,1)}, bf16[384,384]{1,0:T(8,128)(2,1)}, u32[]{:S(2)}, u32[]{:S(2)}) collective-permute-start(bf16[384,384]{1,0:T(8,128)(2,1)} %collective-permute-done.11), channel_id=1, source_target_pairs={{0,12},{4,0},{8,4},{12,8},{1,13},{5,1},{9,5},{13,9},{2,14},{6,2},{... | collective-permute-start | bytes 884744 | tf_op jit(solution)/shard_map/ppermute | solution.py:162
  200.6 34.1 %collective-permute-start.21 = (bf16[4,96,384]{2,1,0:T(8,128)(2,1)}, bf16[4,96,384]{2,1,0:T(8,128)(2,1)}, u32[]{:S(2)}, u32[]{:S(2)}) collective-permute-start(bf16[4,96,384]{2,1,0:T(8,128)(2,1)} %collective-permute-done.20), channel_id=1, source_target_pairs={{0,4},{4,8},{8,12},{12,0},{1,5},{5,9},{9,13},{13,1},{2,6},{6,10},{... | collective-permute-start | bytes 884744 | tf_op jit(solution)/shard_map/ppermute | solution.py:162
  205.9 36.7 %collective-permute-start.14 = (bf16[384,384]{1,0:T(8,128)(2,1)}, bf16[384,384]{1,0:T(8,128)(2,1)}, u32[]{:S(2)}, u32[]{:S(2)}) collective-permute-start(bf16[384,384]{1,0:T(8,128)(2,1)} %collective-permute-done.12), channel_id=1, source_target_pairs={{0,4},{4,8},{8,12},{12,0},{1,5},{5,9},{9,13},{13,1},{2,6},{6,10},{... | collective-permute-start | bytes 884744 | tf_op jit(solution)/shard_map/ppermute | solution.py:162
  212.2 32.2 %collective-permute-start.15 = (bf16[384,384]{1,0:T(8,128)(2,1)}, bf16[384,384]{1,0:T(8,128)(2,1)}, u32[]{:S(2)}, u32[]{:S(2)}) collective-permute-start(bf16[384,384]{1,0:T(8,128)(2,1)} %collective-permute-done.13), channel_id=1, source_target_pairs={{0,12},{4,0},{8,4},{12,8},{1,13},{5,1},{9,5},{13,9},{2,14},{6,2},{... | collective-permute-start | bytes 884744 | tf_op jit(solution)/shard_map/ppermute | solution.py:162
  216.6 25.1 %all-to-all-start.5 = ((bf16[4,384,128]{2,1,0:T(8,128)(2,1)}), bf16[4,384,128]{2,1,0:T(8,128)(2,1)S(1)}, u32[]{:S(2)}, u32[]{:S(2)}) async-start(bf16[4,384,128]{2,1,0:T(8,128)(2,1)} %get-tuple-element.45), calls=%async_computation.5 | async-start | bytes 786432 | tf_op jit(solution)/shard_map/all_to_all | solution.py:207
  234.7 11.5 %collective-permute-start.2 = (bf16[4,4,128]{2,1,0:T(4,128)(2,1)S(1)}, bf16[4,4,128]{2,1,0:T(4,128)(2,1)S(1)}, u32[]{:S(2)}, u32[]{:S(2)}) collective-permute-start(bf16[4,4,128]{2,1,0:T(4,128)(2,1)S(1)} %get-tuple-element.44), channel_id=1, source_target_pairs={{0,1},{1,0},{2,3},{3,2},{4,5},{5,4},{6,7},{7,6},{8,9},{9,8},{10,11... | collective-permute-start | bytes 12296 | tf_op jit(solution)/shard_map/ppermute | solution.py:174
  242.5 4.0 %collective-permute-start = (bf16[512,512]{1,0:T(8,128)(2,1)S(1)}, bf16[512,512]{1,0:T(8,128)(2,1)S(1)}, u32[]{:S(2)}, u32[]{:S(2)}) collective-permute-start(bf16[512,512]{1,0:T(8,128)(2,1)S(1)} %convolution_convert_fusion), channel_id=1, source_target_pairs={{0,1},{1,0},{2,3},{3,2},{4,5},{5,4},{6,7},{7,6},{8,9},{9,8},{10,11... | collective-permute-start | bytes 1572872 | tf_op jit(solution)/shard_map/ppermute | solution.py:174
  246.2 3.7 %collective-permute-start.3 = (bf16[4,4,128]{2,1,0:T(4,128)(2,1)S(1)}, bf16[4,4,128]{2,1,0:T(4,128)(2,1)S(1)}, u32[]{:S(2)}, u32[]{:S(2)}) collective-permute-start(bf16[4,4,128]{2,1,0:T(4,128)(2,1)S(1)} %add_convert_fusion.1), channel_id=1, source_target_pairs={{0,2},{2,0},{1,3},{3,1},{4,6},{6,4},{5,7},{7,5},{8,10},{10,8},{9,1... | collective-permute-start | bytes 12296 | tf_op jit(solution)/shard_map/ppermute | solution.py:174
  246.6 14.3 %collective-permute-start.1 = (bf16[512,512]{1,0:T(8,128)(2,1)S(1)}, bf16[512,512]{1,0:T(8,128)(2,1)S(1)}, u32[]{:S(2)}, u32[]{:S(2)}) collective-permute-start(bf16[512,512]{1,0:T(8,128)(2,1)S(1)} %add_convert_fusion), channel_id=1, source_target_pairs={{0,2},{2,0},{1,3},{3,1},{4,6},{6,4},{5,7},{7,5},{8,10},{10,8},{9,1... | collective-permute-start | bytes 1572872 | tf_op jit(solution)/shard_map/ppermute | solution.py:174
  (13 other events, 56.0 us)
Sparse Core Ops, SparseCore 0:
  11.5 22.3 all-gather.4
  48.2 18.7 all-gather.2

commit v3 on v2

--- a/solution.py
+++ b/solution.py
@@ -16,7 +16,7 @@
 
 def channel_kernel(
     x_ref, cot_ref, up_ref, down_ref, mix_ref, shift_ref,
-    back_ref, reduced_ref, up_grad_ref, down_grad_ref,
+    back_ref, reduced_ref, gate_grad_ref, value_grad_ref, down_grad_ref,
     x_all, cot_all, back_acc, reduced_acc,
 ):
     step = pl.program_id(0)
@@ -69,7 +69,8 @@
                 total = total + mix(g, j, k) * cots[g][j]
             lifted_cot = total.astype(BF16)
             back_acc[k] += dot(up_ref[g, k], lifted_cot, ((0,), (0,)))
-            up_grad_ref[g, k] = dot(lifted_cot, x_all[k], ((1,), (1,))).astype(BF16)
+            grad_ref = (gate_grad_ref, value_grad_ref)[g]
+            grad_ref[k] = dot(lifted_cot, x_all[k], ((1,), (1,))).astype(BF16)
 
     @pl.when(step == pl.num_programs(0) - 1)
     def _():
@@ -92,7 +93,7 @@
     mix = jnp.transpose(up_second, (1, 0, 2, 3)).reshape(hidden, 2 * blocks * blocks).astype(F32)
     shift = jnp.transpose(up_shift, (2, 0, 1)).reshape(hidden, 2 * blocks)
     whole = pl.BlockSpec(x.shape, lambda i: (0, 0, 0, 0))
-    back, reduced, up_grad, down_grad = pl.pallas_call(
+    back, reduced, gate_grad, value_grad, down_grad = pl.pallas_call(
         channel_kernel,
         grid=(hidden // tile,),
         in_specs=[
@@ -106,13 +107,15 @@
         out_specs=[
             whole,
             whole,
-            pl.BlockSpec((2, blocks, tile, chans), lambda i: (0, 0, i, 0)),
+            pl.BlockSpec((blocks, tile, chans), lambda i: (0, i, 0)),
+            pl.BlockSpec((blocks, tile, chans), lambda i: (0, i, 0)),
             pl.BlockSpec((chunks, blocks, chans // chunks, tile), lambda i: (0, 0, 0, i)),
         ],
         out_shape=[
             jax.ShapeDtypeStruct(x.shape, BF16),
             jax.ShapeDtypeStruct(x.shape, BF16),
-            jax.ShapeDtypeStruct((2, blocks, hidden, chans), BF16),
+            jax.ShapeDtypeStruct((blocks, hidden, chans), BF16),
+            jax.ShapeDtypeStruct((blocks, hidden, chans), BF16),
             jax.ShapeDtypeStruct((chunks, blocks, chans // chunks, hidden), BF16),
         ],
         scratch_shapes=[
@@ -135,7 +138,7 @@
         reduced = jnp.swapaxes(reduced.reshape(blocks, shares, part, tokens), 0, 1)
     if chunks != n:
         down_grad = jnp.swapaxes(down_grad.reshape(blocks, n, chans // n, hidden), 0, 1)
-    return back, reduced, up_grad, down_grad
+    return back, reduced, gate_grad, value_grad, down_grad
 
 
 def pieces_sum(x, axes):
@@ -143,26 +146,41 @@
     return jnp.sum(moved.astype(F32), axis=0)
 
 
-def ring_sums(parts, axis):
+def after(values, *others):
+    return lax.optimization_barrier((values, others))[0]
+
+
+def own_rows(rows, axis, way, back):
+    n = lax.axis_size(axis)
+    at = (lax.axis_index(axis) - way * back) % n
+    return lax.dynamic_index_in_dim(rows, at, 0, keepdims=False)
+
+
+def ring_step(held, parts, axis):
+    n = lax.axis_size(axis)
+    return [
+        lax.ppermute(h, axis, [(i, (i + way) % n) for i in range(n)])
+        for h, (_, way) in zip(held, parts)
+    ]
+
+
+def ring_reduce(held, parts, axis, first, last):
+    for s in range(first, last):
+        held = [
+            (h.astype(F32) + own_rows(rows, axis, way, s + 2).astype(F32)).astype(BF16)
+            for h, (rows, way) in zip(ring_step(held, parts, axis), parts)
+        ]
+    return held
+
+
+def ring_gather(pieces, parts, axis, first, last):
     n = lax.axis_size(axis)
     me = lax.axis_index(axis)
-    perms = {way: [(i, (i + way) % n) for i in range(n)] for way in (1, -1)}
-
-    def own(rows, way, back):
-        return lax.dynamic_index_in_dim(rows, (me - way * back) % n, 0, keepdims=False)
-
-    held = [own(rows, way, 1) for rows, way in parts]
-    for s in range(n - 1):
-        held = [
-            (lax.ppermute(h, axis, perms[way]).astype(F32) + own(rows, way, s + 2).astype(F32)).astype(BF16)
-            for h, (rows, way) in zip(held, parts)
-        ]
-    pieces = [[(me, h)] for h in held]
-    for s in range(n - 1):
-        held = [lax.ppermute(h, axis, perms[way]) for h, (_, way) in zip(held, parts)]
+    held = [p[-1][1] for p in pieces]
+    for s in range(first, last):
+        held = ring_step(held, parts, axis)
         for got, h, (_, way) in zip(pieces, held, parts):
             got.append(((me - way * (s + 1)) % n, h))
-    return pieces
 
 
 def swap_sum(x):
@@ -226,35 +244,35 @@
     seq_out = (input_tokens + gating * mixed_float).astype(BF16)
     block_in = seq_out.reshape(blocks, part, length)
     x_all = lax.all_gather(block_in, PLANE, axis=0)
-    back, reduced, up_grad, down_grad = channel_block(
+    back, reduced, gate_grad, value_grad, down_grad = channel_block(
         x_all, cot_all, up_first, up_second, up_shift, down_first
     )
-    up_rows = up_grad.reshape(2, n, -1, up_grad.shape[-1])
-    gate_pieces, value_pieces, down_pieces = ring_sums(
-        [(up_rows[0], 1), (up_rows[1], -1), (down_grad, 1)], "seq"
-    )
-    up_first_grad = jnp.zeros(up_rows.shape, F32)
-    for s in range(n):
-        for g, pieces in enumerate((gate_pieces, value_pieces)):
-            at, piece = pieces[s]
-            up_first_grad = lax.dynamic_update_slice(
-                up_first_grad, piece.astype(F32)[None, None], (g, at, 0, 0)
-            )
-    up_first_grad = up_first_grad.reshape(up_grad.shape)
-    share = down_grad.shape[2]
-    down_first_grad = jnp.zeros((n * share,) + (blocks, down_grad.shape[3]), F32)
-    for at, piece in down_pieces:
-        turned = lax.optimization_barrier(jnp.swapaxes(piece, 0, 1).astype(F32))
-        down_first_grad = lax.dynamic_update_slice(down_first_grad, turned, (at * share, 0, 0))
+    chans = gate_grad.shape[-1]
+    parts = [
+        (gate_grad.reshape(n, -1, chans), 1),
+        (value_grad.reshape(n, -1, chans), -1),
+        (down_grad, 1),
+    ]
+    held = [own_rows(rows_, "seq", way, 1) for rows_, way in parts]
+    held = ring_reduce(held, parts, "seq", 0, 1)
 
     input_cot = pieces_sum(back, PLANE).reshape(rows, length)
     total_cot = cotangent.reshape(rows, length).astype(F32) + input_cot
+    held = ring_reduce(after(held, input_cot), parts, "seq", 1, n - 1)
     mixed_cot = (total_cot * gating).astype(BF16)
     straight = total_cot + total_cot * mixed_float * gating * (1.0 - gating) * scale
-    cots = to_positions(mixed_cot).astype(F32)
+    moved_cots = to_positions(mixed_cot)
+    cots = moved_cots.astype(F32)
+    held = after(held, moved_cots)
+    reduced = after(reduced, moved_cots)
+    pieces = [[(lax.axis_index("seq"), h)] for h in held]
+    ring_gather(pieces, parts, "seq", 0, 1)
     section_spread = jnp.sum(left[:, :, None, :] * cots[:, None], axis=0).astype(BF16)
     left_grad = jnp.sum(cots[:, None] * sections.astype(F32)[None], axis=2)
     section_cot = to_blocks(section_spread)
+    for p in pieces:
+        p[-1] = (p[-1][0], after(p[-1][1], section_cot))
+    ring_gather(pieces, parts, "seq", 1, n - 1)
     right_grad = dot(section_cot, flat, ((0,), (0,)))
     token_grad = straight + dot(section_cot, right, ((1,), (0,)))
 
@@ -266,6 +284,19 @@
             for k in range(blocks)
         ]
     ).astype(BF16)
+    up_first_grad = jnp.zeros((2,) + parts[0][0].shape, F32)
+    for s in range(n):
+        for g in range(2):
+            at, piece = pieces[g][s]
+            up_first_grad = lax.dynamic_update_slice(
+                up_first_grad, piece.astype(F32)[None, None], (g, at, 0, 0)
+            )
+    up_first_grad = up_first_grad.reshape((2,) + gate_grad.shape)
+    share = down_grad.shape[2]
+    down_first_grad = jnp.zeros((n * share,) + (blocks, down_grad.shape[3]), F32)
+    for at, piece in pieces[2]:
+        turned = lax.optimization_barrier(jnp.swapaxes(piece, 0, 1).astype(F32))
+        down_first_grad = lax.dynamic_update_slice(down_first_grad, turned, (at * share, 0, 0))
     left_grad = jnp.transpose(swap_sum(left_grad), (2, 0, 1))
     right_grad = swap_sum(right_grad)
     return (

time: 270 us -> 265 us (0.981)
  starting transfers between devices: 64.9 us -> 52.1 us
  other arithmetic: 41.9 us -> 54.4 us
  waiting for transfers between devices: 88.7 us -> 80.3 us
    all_to_all x1, starting transfers between devices: 16.3 us -> 5.08 us  [to_blocks(): x = lax.all_to_all(x, 'seq', split_axis=0, concat_axis=0, tiled=True)]
    ppermute x4, waiting for transfers between devices: 9.45 us -> 0.01 us  [swap_sum(): got = lax.ppermute(sent, axis, [(i, i ^ bit) for i in range(n)])]
    convert_element_type x7 -> x10, other arithmetic: 4.01 us -> 12.5 us  [the longest x9 11.4 us: ring_reduce(): (h.astype(F32) + own_rows(rows, axis, way, s + 2).astype(F32)).astype(BF16)]
    all_to_all x2, waiting for transfers between devices: 8.03 us -> 0.01 us  [pieces_sum(): moved = lax.all_to_all(x, axes, split_axis=0, concat_axis=0, tiled=True)]
    all_to_all x2, waiting for transfers between devices: 11.7 us -> 17.8 us  [to_positions(): return lax.all_to_all(x, 'seq', split_axis=0, concat_axis=0, tiled=True)]
    ppermute x18, starting transfers between devices: 26.8 us -> 23.6 us  [ring_step(): lax.ppermute(h, axis, [(i, (i + way) % n) for i in range(n)])]
    slice x1 -> x0, local copies, waits for them, and re-layouts: 3.03 us -> none  [per_device(): up_rows[1]]
    unnamed x34 -> x58, local copies, waits for them, and re-layouts: 5.15 us -> 7.81 us
  transfers between devices with their start and end apart: 29 -> 29, of which waited for: 16 -> 16; matrix products, arithmetic and copies ran while one was open for 22% -> 28% of each run, Pallas kernels for 0% -> 0%
where the time goes in v3:
time: 265 us; the launch traced here: 263 us
  waiting for transfers between devices  80.3 us (30%)
  other arithmetic  54.4 us (21%)
  starting transfers between devices  52.1 us (20%)
  local copies, waits for them, and re-layouts  27.2 us (10%)
  Pallas kernels  18.5 us (7%)
  between operations  14.7 us (6%)
  blocking collectives  13.3 us (5%)
  matrix products  2.72 us (1%)
    ppermute x18, waiting for transfers between devices, ring_step(): lax.ppermute(h, axis, [(i, (i + way) % n) for i in range(n)])  42.5 us
    ppermute x18, starting transfers between devices, ring_step(): lax.ppermute(h, axis, [(i, (i + way) % n) for i in range(n)])  23.6 us
    pallas_call x1, Pallas kernels, channel_block(): pl.pallas_call(channel_kernel, grid=(hidden // tile,), in_specs=[whole, w...  18.5 us
    all_to_all x2, waiting for transfers between devices, to_positions(): return lax.all_to_all(x, 'seq', split_axis=0, concat_axis=0, tiled=True)  17.8 us
    all_gather x1, waiting for transfers between devices, per_device(): x_all = lax.all_gather(block_in, PLANE, axis=0)  15.2 us
    dynamic_update_slice x8, other arithmetic, per_device(): lax.dynamic_update_slice(up_first_grad, piece.astype(F32)[None, None], (g...  14.6 us
    all_to_all x1, blocking collectives, to_blocks(): x = lax.all_to_all(x, 'seq', split_axis=0, concat_axis=0, tiled=True)  13.3 us
    all_to_all x2, starting transfers between devices, to_positions(): return lax.all_to_all(x, 'seq', split_axis=0, concat_axis=0, tiled=True)  11.5 us
  transfers between devices with their start and end apart: 29, of which 16 were waited for; matrix products, arithmetic and copies ran while one was open for 28% of the time, Pallas kernels for 0%

profile of v3, /device:TPU:0, one launch (start us, length us, event | category | flops | bytes accessed | tf_op | source)
XLA Modules:
  0.0 263.1 jit_solution(18296228882625869532)
XLA Ops:
  12.9 6.3 %all-to-all-start = ((bf16[4,384,128]{2,1,0:T(8,128)(2,1)}), bf16[4,384,128]{2,1,0:T(8,128)(2,1)S(1)}, u32[]{:S(2)}, u32[]{:S(2)}) async-start(bf16[4,384,128]{2,1,0:T(8,128)(2,1)} %bitcast.256), calls=%async_computation | async-start | bytes 786432 | tf_op jit(solution)/shard_map/all_to_all | solution.py:222
  19.2 11.7 %all-to-all-done = bf16[4,384,128]{2,1,0:T(8,128)(2,1)S(1)} async-done(((bf16[4,384,128]{2,1,0:T(8,128)(2,1)}), bf16[4,384,128]{2,1,0:T(8,128)(2,1)S(1)}, u32[]{:S(2)}, u32[]{:S(2)}) %all-to-all-start) | async-done | bytes 393248 | tf_op jit(solution)/shard_map/all_to_all | solution.py:222
  32.1 13.3 %all_to_all.30 = bf16[4,384,128]{2,1,0:T(8,128)(2,1)S(1)} all-to-all(bf16[4,384,128]{2,1,0:T(8,128)(2,1)S(1)} %multiply_reduce_fusion.2), channel_id=1, replica_groups=mesh['grp'=2,'seq'=4,'ch'=2,'sub'=2] {'seq'}, dimensions={0} | all-to-all | bytes 786432 | tf_op jit(solution)/shard_map/all_to_all | solution.py:225
  48.4 3.4 %copy.68 = bf16[384,4,384]{0,2,1:T(8,128)(2,1)} copy(bf16[384,4,384]{2,1,0:T(4,128)(2,1)} %param.19) | data formatting | bytes 2359296 | tf_op args[8]
  52.1 15.2 %all-gather.3.cloned.1.call-done.x_ref = bf16[4,4,96,512]{3,2,1,0:T(8,128)(2,1)} async-done(((bf16[1,4,96,512]{3,2,1,0:T(8,128)(2,1)}), bf16[4,4,96,512]{3,2,1,0:T(8,128)(2,1)}) %all-gather.3.cloned.1.call-update) | async-done | bytes 1572880 | tf_op jit(solution)/shard_map/all_gather | solution.py:246
  67.3 18.5 %shard_map.154 = (bf16[4,4,96,512]{3,2,1,0:T(8,128)(2,1)}, bf16[4,4,96,512]{3,2,1,0:T(8,128)(2,1)}, bf16[4,384,384]{2,1,0:T(8,128)(2,1)S(1)}, bf16[4,384,384]{2,...) custom-call(bf16[4,4,96,512]{3,2,1,0:T(8,128)(2,1)} %all-gather.3.cloned.1.call-done.x_ref, ...), custom_call_target="tpu_custom_call" | custom-call | flops 5435817984 | bytes 14680064 | tf_op jit(solution)/shard_map/pallas_call | solution.py:96
  90.6 2.4 collective-permute-start.5
  93.0 6.6 %collective-permute-done.4 = bf16[384,384]{1,0:T(8,128)(2,1)} collective-permute-done((bf16[384,384]{1,0:T(8,128)(2,1)}, bf16[384,384]{1,0:T(8,128)(2,1)}, u32[]{:S(2)}, u32[]{:S(2)}) %collective-permute-start.4) | collective-permute-done | bytes 294944 | tf_op jit(solution)/shard_map/ppermute | solution.py:162
  101.5 4.3 %collective-permute-done.6 = bf16[4,96,384]{2,1,0:T(8,128)(2,1)S(1)} collective-permute-done((bf16[4,96,384]{2,1,0:T(8,128)(2,1)S(1)}, bf16[4,96,384]{2,1,0:T(8,128)(2,1)S(1)}, u32[]{:S(2)}, u32[]{:S(2)}) %collective-permute-start.6) | collective-permute-done | bytes 294944 | tf_op jit(solution)/shard_map/ppermute | solution.py:162
  106.5 4.8 %collective-permute-done.5 = bf16[384,384]{1,0:T(8,128)(2,1)S(1)} collective-permute-done((bf16[384,384]{1,0:T(8,128)(2,1)S(1)}, bf16[384,384]{1,0:T(8,128)(2,1)S(1)}, u32[]{:S(2)}, u32[]{:S(2)}) %collective-permute-start.5) | collective-permute-done | bytes 294944 | tf_op jit(solution)/shard_map/ppermute | solution.py:162
  116.0 2.3 reshape.1235
  118.2 4.3 %all-to-all-start.2 = ((bf16[4,4,96,512]{3,2,1,0:T(8,128)(2,1)}), bf16[4,4,96,512]{3,2,1,0:T(8,128)(2,1)}, u32[]{:S(2)}, u32[]{:S(2)}) async-start(bf16[4,4,96,512]{3,2,1,0:T(8,128)(2,1)} %get-tuple-element.22), calls=%async_computation.2 | async-start | bytes 3145728 | tf_op jit(solution)/shard_map/all_to_all | solution.py:145
  122.6 3.3 %collective-permute-start.9 = (bf16[384,384]{1,0:T(8,128)(2,1)}, bf16[384,384]{1,0:T(8,128)(2,1)S(1)}, u32[]{:S(2)}, u32[]{:S(2)}) collective-permute-start(bf16[384,384]{1,0:T(8,128)(2,1)} %fusion.26), channel_id=1, source_target_pairs={{0,12},{4,0},{8,4},{12,8},{1,13},{5,1},{9,5},{13,9},{2,14},{6,2},{... | collective-permute-start | bytes 884744 | tf_op jit(solution)/shard_map/ppermute | solution.py:162
  125.9 2.2 fusion.6
  129.3 4.3 %collective-permute-done.9 = bf16[384,384]{1,0:T(8,128)(2,1)S(1)} collective-permute-done((bf16[384,384]{1,0:T(8,128)(2,1)}, bf16[384,384]{1,0:T(8,128)(2,1)S(1)}, u32[]{:S(2)}, u32[]{:S(2)}) %collective-permute-start.9) | collective-permute-done | bytes 294944 | tf_op jit(solution)/shard_map/ppermute | solution.py:162
  134.4 4.2 %collective-permute-start.10 = (bf16[384,384]{1,0:T(8,128)(2,1)}, bf16[384,384]{1,0:T(8,128)(2,1)}, u32[]{:S(2)}, u32[]{:S(2)}) collective-permute-start(bf16[384,384]{1,0:T(8,128)(2,1)} %fusion.22), channel_id=1, source_target_pairs={{0,12},{4,0},{8,4},{12,8},{1,13},{5,1},{9,5},{13,9},{2,14},{6,2},{... | collective-permute-start | bytes 884744 | tf_op jit(solution)/shard_map/ppermute | solution.py:162
  143.1 3.5 %collective-permute-done.8 = bf16[384,384]{1,0:T(8,128)(2,1)S(1)} collective-permute-done((bf16[384,384]{1,0:T(8,128)(2,1)S(1)}, bf16[384,384]{1,0:T(8,128)(2,1)S(1)}, u32[]{:S(2)}, u32[]{:S(2)}) %collective-permute-start.8) | collective-permute-done | bytes 294944 | tf_op jit(solution)/shard_map/ppermute | solution.py:162
  148.4 2.6 convert_reduce_fusion.1
  151.0 2.3 reshape.1221
  153.3 2.7 %fusion.30 = bf16[4,384,128]{2,0,1:T(4,128)(2,1)S(1)} fusion(f32[384]{0:T(512)S(1)} %add.456, f32[384,4,128]{2,1,0:T(4,128)} %reshape.1235, f32[384]{0:T(512)S(1)} %mul.582, f32[384,4,128]{2,1,0:T(4,128)} %reshape.1234, f32[384,4,128]{2,1,0:T(4,128)} %reshape.1221), kind=kLoop, calls=%fused_computation.79 | loop fusion | flops 1572864 | bytes 2755584 | tf_op jit(solution)/shard_map/transpose | solution.py:221
  156.8 5.1 %all-to-all-start.3 = ((bf16[4,384,128]{2,1,0:T(8,128)(2,1)}), bf16[4,384,128]{2,1,0:T(8,128)(2,1)}, u32[]{:S(2)}, u32[]{:S(2)}) async-start(bf16[4,384,128]{2,1,0:T(8,128)(2,1)} %copy.71), calls=%async_computation.3 | async-start | bytes 786432 | tf_op jit(solution)/shard_map/all_to_all | solution.py:222
  165.5 2.2 bitcast_add_fusion
  167.7 6.1 %all-to-all-done.3 = bf16[4,384,128]{2,1,0:T(8,128)(2,1)} async-done(((bf16[4,384,128]{2,1,0:T(8,128)(2,1)}), bf16[4,384,128]{2,1,0:T(8,128)(2,1)}, u32[]{:S(2)}, u32[]{:S(2)}) %all-to-all-start.3) | async-done | bytes 393248 | tf_op jit(solution)/shard_map/all_to_all | solution.py:222
  177.3 5.1 %all-to-all-start.5 = ((bf16[4,384,128]{2,1,0:T(8,128)(2,1)}), bf16[4,384,128]{2,1,0:T(8,128)(2,1)S(1)}, u32[]{:S(2)}, u32[]{:S(2)}) async-start(bf16[4,384,128]{2,1,0:T(8,128)(2,1)} %get-tuple-element.67), calls=%async_computation.5 | async-start | bytes 786432 | tf_op jit(solution)/shard_map/all_to_all | solution.py:225
  187.0 2.8 %broadcast_in_dim.64 = f32[2,4,384,384]{3,2,1,0:T(8,128)} broadcast(f32[]{:T(128)} %constant.118.clone.1), dimensions={} | broadcast | bytes 4718596 | tf_op jit(solution)/shard_map/broadcast_in_dim | solution.py:287
  196.0 4.7 %all-to-all-done.5 = bf16[4,384,128]{2,1,0:T(8,128)(2,1)S(1)} async-done(((bf16[4,384,128]{2,1,0:T(8,128)(2,1)}), bf16[4,384,128]{2,1,0:T(8,128)(2,1)S(1)}, u32[]{:S(2)}, u32[]{:S(2)}) %all-to-all-start.5) | async-done | bytes 393248 | tf_op jit(solution)/shard_map/all_to_all | solution.py:225
  201.5 3.6 %all-to-all-start.4 = ((bf16[4,4,96,512]{3,2,1,0:T(8,128)(2,1)}), bf16[4,4,96,512]{3,2,1,0:T(8,128)(2,1)S(1)}, u32[]{:S(2)}, u32[]{:S(2)}) async-start(bf16[4,4,96,512]{3,2,1,0:T(8,128)(2,1)} %get-tuple-element.23), calls=%async_computation.4 | async-start | bytes 3145728 | tf_op jit(solution)/shard_map/all_to_all | solution.py:145
  212.4 3.9 %collective-permute-start.16 = (bf16[384,384]{1,0:T(8,128)(2,1)}, bf16[384,384]{1,0:T(8,128)(2,1)}, u32[]{:S(2)}, u32[]{:S(2)}) collective-permute-start(bf16[384,384]{1,0:T(8,128)(2,1)} %collective-permute-done.14), channel_id=1, source_target_pairs={{0,12},{4,0},{8,4},{12,8},{1,13},{5,1},{9,5},{13,9},{2,14},{6,2},{... | collective-permute-start | bytes 884744 | tf_op jit(solution)/shard_map/ppermute | solution.py:162
  222.1 5.1 %collective-permute-done.15 = bf16[384,384]{1,0:T(8,128)(2,1)} collective-permute-done((bf16[384,384]{1,0:T(8,128)(2,1)}, bf16[384,384]{1,0:T(8,128)(2,1)}, u32[]{:S(2)}, u32[]{:S(2)}) %collective-permute-start.15) | collective-permute-done | bytes 294944 | tf_op jit(solution)/shard_map/ppermute | solution.py:162
  229.1 4.3 %collective-permute-done.16 = bf16[384,384]{1,0:T(8,128)(2,1)} collective-permute-done((bf16[384,384]{1,0:T(8,128)(2,1)}, bf16[384,384]{1,0:T(8,128)(2,1)}, u32[]{:S(2)}, u32[]{:S(2)}) %collective-permute-start.16) | collective-permute-done | bytes 294944 | tf_op jit(solution)/shard_map/ppermute | solution.py:162
  241.1 5.2 %collective-permute-done.17 = bf16[384,384]{1,0:T(8,128)(2,1)} collective-permute-done((bf16[384,384]{1,0:T(8,128)(2,1)}, bf16[384,384]{1,0:T(8,128)(2,1)}, u32[]{:S(2)}, u32[]{:S(2)}) %collective-permute-start.17) | collective-permute-done | bytes 294944 | tf_op jit(solution)/shard_map/ppermute | solution.py:162
  249.8 2.3 collective-permute-done.18
  (161 shorter events, 79.8 us)
Async XLA Ops:
  7.2 44.9 %all-gather.5.cloned.1.call-start = ((), (), s32[]{:S(2)}) async-start(), calls=%async_computation.7 | async-start | bytes 1966080 | tf_op jit(solution)/shard_map/all_gather | solution.py:237
  12.9 18.0 %all-to-all-start = ((bf16[4,384,128]{2,1,0:T(8,128)(2,1)}), bf16[4,384,128]{2,1,0:T(8,128)(2,1)S(1)}, u32[]{:S(2)}, u32[]{:S(2)}) async-start(bf16[4,384,128]{2,1,0:T(8,128)(2,1)} %bitcast.256), calls=%async_computation | async-start | bytes 786432 | tf_op jit(solution)/shard_map/all_to_all | solution.py:222
  19.2 48.1 %all-gather.3.cloned.1.call-start = ((), (), s32[]{:S(2)}) async-start(), calls=%async_computation.6 | async-start | bytes 1966080 | tf_op jit(solution)/shard_map/all_gather | solution.py:246
  85.7 26.9 %copy-start.3 = (bf16[4,96,1,512]{3,1,2,0:T(8,128)(2,1)S(1)}, bf16[4,96,1,512]{3,1,2,0:T(8,128)(2,1)}, u32[]{:S(2)}) copy-start(bf16[4,96,1,512]{3,1,2,0:T(8,128)(2,1)} %param.11) | copy-start | bytes 1179652
  87.5 12.1 %collective-permute-start.4 = (bf16[384,384]{1,0:T(8,128)(2,1)}, bf16[384,384]{1,0:T(8,128)(2,1)}, u32[]{:S(2)}, u32[]{:S(2)}) collective-permute-start(bf16[384,384]{1,0:T(8,128)(2,1)} %dynamic-slice_bitcast_fusion.2), channel_id=1, source_target_pairs={{0,4},{4,8},{8,12},{12,0},{1,5},{5,9},{9,13},{13,1},{2,6},{6,10},{... | collective-permute-start | bytes 884744 | tf_op jit(solution)/shard_map/ppermute | solution.py:162
  89.0 16.7 %collective-permute-start.6 = (bf16[4,96,384]{2,1,0:T(8,128)(2,1)S(1)}, bf16[4,96,384]{2,1,0:T(8,128)(2,1)S(1)}, u32[]{:S(2)}, u32[]{:S(2)}) collective-permute-start(bf16[4,96,384]{2,1,0:T(8,128)(2,1)S(1)} %dynamic-slice_bitcast_fusion), channel_id=1, source_target_pairs={{0,4},{4,8},{8,12},{12,0},{1,5},{5,9},{9,13},{13,1},{2,6},{6,10},{... | collective-permute-start | bytes 884744 | tf_op jit(solution)/shard_map/ppermute | solution.py:162
  90.6 20.7 %collective-permute-start.5 = (bf16[384,384]{1,0:T(8,128)(2,1)S(1)}, bf16[384,384]{1,0:T(8,128)(2,1)S(1)}, u32[]{:S(2)}, u32[]{:S(2)}) collective-permute-start(bf16[384,384]{1,0:T(8,128)(2,1)S(1)} %dynamic-slice_bitcast_fusion.1), channel_id=1, source_target_pairs={{0,12},{4,0},{8,4},{12,8},{1,13},{5,1},{9,5},{13,9},{2,14},{6,2},{... | collective-permute-start | bytes 884744 | tf_op jit(solution)/shard_map/ppermute | solution.py:162
  112.1 16.0 %collective-permute-start.7 = (bf16[384,384]{1,0:T(8,128)(2,1)}, bf16[384,384]{1,0:T(8,128)(2,1)}, u32[]{:S(2)}, u32[]{:S(2)}) collective-permute-start(bf16[384,384]{1,0:T(8,128)(2,1)} %fusion.27), channel_id=1, source_target_pairs={{0,4},{4,8},{8,12},{12,0},{1,5},{5,9},{9,13},{13,1},{2,6},{6,10},{... | collective-permute-start | bytes 884744 | tf_op jit(solution)/shard_map/ppermute | solution.py:162
  118.2 30.2 %all-to-all-start.2 = ((bf16[4,4,96,512]{3,2,1,0:T(8,128)(2,1)}), bf16[4,4,96,512]{3,2,1,0:T(8,128)(2,1)}, u32[]{:S(2)}, u32[]{:S(2)}) async-start(bf16[4,4,96,512]{3,2,1,0:T(8,128)(2,1)} %get-tuple-element.22), calls=%async_computation.2 | async-start | bytes 3145728 | tf_op jit(solution)/shard_map/all_to_all | solution.py:145
  122.6 11.1 %collective-permute-start.9 = (bf16[384,384]{1,0:T(8,128)(2,1)}, bf16[384,384]{1,0:T(8,128)(2,1)S(1)}, u32[]{:S(2)}, u32[]{:S(2)}) collective-permute-start(bf16[384,384]{1,0:T(8,128)(2,1)} %fusion.26), channel_id=1, source_target_pairs={{0,12},{4,0},{8,4},{12,8},{1,13},{5,1},{9,5},{13,9},{2,14},{6,2},{... | collective-permute-start | bytes 884744 | tf_op jit(solution)/shard_map/ppermute | solution.py:162
  128.1 12.3 %collective-permute-start.11 = (bf16[4,96,384]{2,1,0:T(8,128)(2,1)}, bf16[4,96,384]{2,1,0:T(8,128)(2,1)S(1)}, u32[]{:S(2)}, u32[]{:S(2)}) collective-permute-start(bf16[4,96,384]{2,1,0:T(8,128)(2,1)} %fusion.25), channel_id=1, source_target_pairs={{0,4},{4,8},{8,12},{12,0},{1,5},{5,9},{9,13},{13,1},{2,6},{6,10},{... | collective-permute-start | bytes 884744 | tf_op jit(solution)/shard_map/ppermute | solution.py:162
  129.3 17.4 %collective-permute-start.8 = (bf16[384,384]{1,0:T(8,128)(2,1)S(1)}, bf16[384,384]{1,0:T(8,128)(2,1)S(1)}, u32[]{:S(2)}, u32[]{:S(2)}) collective-permute-start(bf16[384,384]{1,0:T(8,128)(2,1)S(1)} %fusion.24), channel_id=1, source_target_pairs={{0,4},{4,8},{8,12},{12,0},{1,5},{5,9},{9,13},{13,1},{2,6},{6,10},{... | collective-permute-start | bytes 884744 | tf_op jit(solution)/shard_map/ppermute | solution.py:162
  134.4 29.3 %collective-permute-start.10 = (bf16[384,384]{1,0:T(8,128)(2,1)}, bf16[384,384]{1,0:T(8,128)(2,1)}, u32[]{:S(2)}, u32[]{:S(2)}) collective-permute-start(bf16[384,384]{1,0:T(8,128)(2,1)} %fusion.22), channel_id=1, source_target_pairs={{0,12},{4,0},{8,4},{12,8},{1,13},{5,1},{9,5},{13,9},{2,14},{6,2},{... | collective-permute-start | bytes 884744 | tf_op jit(solution)/shard_map/ppermute | solution.py:162
  141.2 20.8 %collective-permute-start.12 = (bf16[4,96,384]{2,1,0:T(8,128)(2,1)}, bf16[4,96,384]{2,1,0:T(8,128)(2,1)}, u32[]{:S(2)}, u32[]{:S(2)}) collective-permute-start(bf16[4,96,384]{2,1,0:T(8,128)(2,1)} %fusion.20), channel_id=1, source_target_pairs={{0,4},{4,8},{8,12},{12,0},{1,5},{5,9},{9,13},{13,1},{2,6},{6,10},{... | collective-permute-start | bytes 884744 | tf_op jit(solution)/shard_map/ppermute | solution.py:162
  156.8 17.0 %all-to-all-start.3 = ((bf16[4,384,128]{2,1,0:T(8,128)(2,1)}), bf16[4,384,128]{2,1,0:T(8,128)(2,1)}, u32[]{:S(2)}, u32[]{:S(2)}) async-start(bf16[4,384,128]{2,1,0:T(8,128)(2,1)} %copy.71), calls=%async_computation.3 | async-start | bytes 786432 | tf_op jit(solution)/shard_map/all_to_all | solution.py:222
  163.7 12.3 %copy-start.5 = (f32[4,384,128]{2,1,0:T(8,128)S(1)}, f32[4,384,128]{2,1,0:T(8,128)}, u32[]{:S(2)}) copy-start(f32[4,384,128]{2,1,0:T(8,128)} %copy-done.4) | copy-start | bytes 2359300
  174.9 34.0 %collective-permute-start.19 = (bf16[4,96,384]{2,1,0:T(8,128)(2,1)}, bf16[4,96,384]{2,1,0:T(8,128)(2,1)}, u32[]{:S(2)}, u32[]{:S(2)}) collective-permute-start(bf16[4,96,384]{2,1,0:T(8,128)(2,1)} %fusion.19), channel_id=1, source_target_pairs={{0,4},{4,8},{8,12},{12,0},{1,5},{5,9},{9,13},{13,1},{2,6},{6,10},{... | collective-permute-start | bytes 884744 | tf_op jit(solution)/shard_map/ppermute | solution.py:162
  177.3 23.5 %all-to-all-start.5 = ((bf16[4,384,128]{2,1,0:T(8,128)(2,1)}), bf16[4,384,128]{2,1,0:T(8,128)(2,1)S(1)}, u32[]{:S(2)}, u32[]{:S(2)}) async-start(bf16[4,384,128]{2,1,0:T(8,128)(2,1)} %get-tuple-element.67), calls=%async_computation.5 | async-start | bytes 786432 | tf_op jit(solution)/shard_map/all_to_all | solution.py:225
  182.3 9.2 %collective-permute-start.2 = (bf16[4,4,128]{2,1,0:T(4,128)(2,1)S(1)}, bf16[4,4,128]{2,1,0:T(4,128)(2,1)S(1)}, u32[]{:S(2)}, u32[]{:S(2)}) collective-permute-start(bf16[4,4,128]{2,1,0:T(4,128)(2,1)S(1)} %get-tuple-element.66), channel_id=1, source_target_pairs={{0,1},{1,0},{2,3},{3,2},{4,5},{5,4},{6,7},{7,6},{8,9},{9,8},{10,11... | collective-permute-start | bytes 12296 | tf_op jit(solution)/shard_map/ppermute | solution.py:192
  182.3 27.7 %collective-permute-start.13 = (bf16[384,384]{1,0:T(8,128)(2,1)}, bf16[384,384]{1,0:T(8,128)(2,1)}, u32[]{:S(2)}, u32[]{:S(2)}) collective-permute-start(bf16[384,384]{1,0:T(8,128)(2,1)} %fusion.23), channel_id=1, source_target_pairs={{0,4},{4,8},{8,12},{12,0},{1,5},{5,9},{9,13},{13,1},{2,6},{6,10},{... | collective-permute-start | bytes 884744 | tf_op jit(solution)/shard_map/ppermute | solution.py:162
  184.4 28.0 %collective-permute-start.14 = (bf16[384,384]{1,0:T(8,128)(2,1)}, bf16[384,384]{1,0:T(8,128)(2,1)}, u32[]{:S(2)}, u32[]{:S(2)}) collective-permute-start(bf16[384,384]{1,0:T(8,128)(2,1)} %fusion.21), channel_id=1, source_target_pairs={{0,12},{4,0},{8,4},{12,8},{1,13},{5,1},{9,5},{13,9},{2,14},{6,2},{... | collective-permute-start | bytes 884744 | tf_op jit(solution)/shard_map/ppermute | solution.py:162
  191.6 15.4 %copy-start.6 = (f32[4,48,8,128]{3,2,1,0:T(8,128)S(1)}, f32[4,48,8,128]{3,2,1,0:T(8,128)}, u32[]{:S(2)}) copy-start(f32[4,48,8,128]{3,2,1,0:T(8,128)} %get-tuple-element.72) | copy-start | bytes 2359300
  191.6 3.8 %collective-permute-start.3 = (bf16[4,4,128]{2,1,0:T(4,128)(2,1)S(1)}, bf16[4,4,128]{2,1,0:T(4,128)(2,1)S(1)}, u32[]{:S(2)}, u32[]{:S(2)}) collective-permute-start(bf16[4,4,128]{2,1,0:T(4,128)(2,1)S(1)} %add_convert_fusion.1), channel_id=1, source_target_pairs={{0,2},{2,0},{1,3},{3,1},{4,6},{6,4},{5,7},{7,5},{8,10},{10,8},{9,1... | collective-permute-start | bytes 12296 | tf_op jit(solution)/shard_map/ppermute | solution.py:192
  201.5 37.4 %all-to-all-start.4 = ((bf16[4,4,96,512]{3,2,1,0:T(8,128)(2,1)}), bf16[4,4,96,512]{3,2,1,0:T(8,128)(2,1)S(1)}, u32[]{:S(2)}, u32[]{:S(2)}) async-start(bf16[4,4,96,512]{3,2,1,0:T(8,128)(2,1)} %get-tuple-element.23), calls=%async_computation.4 | async-start | bytes 3145728 | tf_op jit(solution)/shard_map/all_to_all | solution.py:145
  208.9 12.2 %collective-permute-start.20 = (bf16[4,96,384]{2,1,0:T(8,128)(2,1)}, bf16[4,96,384]{2,1,0:T(8,128)(2,1)}, u32[]{:S(2)}, u32[]{:S(2)}) collective-permute-start(bf16[4,96,384]{2,1,0:T(8,128)(2,1)} %collective-permute-done.19), channel_id=1, source_target_pairs={{0,4},{4,8},{8,12},{12,0},{1,5},{5,9},{9,13},{13,1},{2,6},{6,10},{... | collective-permute-start | bytes 884744 | tf_op jit(solution)/shard_map/ppermute | solution.py:162
  210.0 17.3 %collective-permute-start.15 = (bf16[384,384]{1,0:T(8,128)(2,1)}, bf16[384,384]{1,0:T(8,128)(2,1)}, u32[]{:S(2)}, u32[]{:S(2)}) collective-permute-start(bf16[384,384]{1,0:T(8,128)(2,1)} %collective-permute-done.13), channel_id=1, source_target_pairs={{0,4},{4,8},{8,12},{12,0},{1,5},{5,9},{9,13},{13,1},{2,6},{6,10},{... | collective-permute-start | bytes 884744 | tf_op jit(solution)/shard_map/ppermute | solution.py:162
  212.4 21.1 %collective-permute-start.16 = (bf16[384,384]{1,0:T(8,128)(2,1)}, bf16[384,384]{1,0:T(8,128)(2,1)}, u32[]{:S(2)}, u32[]{:S(2)}) collective-permute-start(bf16[384,384]{1,0:T(8,128)(2,1)} %collective-permute-done.14), channel_id=1, source_target_pairs={{0,12},{4,0},{8,4},{12,8},{1,13},{5,1},{9,5},{13,9},{2,14},{6,2},{... | collective-permute-start | bytes 884744 | tf_op jit(solution)/shard_map/ppermute | solution.py:162
  219.8 17.0 %collective-permute-start = (bf16[512,512]{1,0:T(8,128)(2,1)S(1)}, bf16[512,512]{1,0:T(8,128)(2,1)S(1)}, u32[]{:S(2)}, u32[]{:S(2)}) collective-permute-start(bf16[512,512]{1,0:T(8,128)(2,1)S(1)} %convolution_convert_fusion), channel_id=1, source_target_pairs={{0,1},{1,0},{2,3},{3,2},{4,5},{5,4},{6,7},{7,6},{8,9},{9,8},{10,11... | collective-permute-start | bytes 1572872 | tf_op jit(solution)/shard_map/ppermute | solution.py:192
  222.1 18.0 %collective-permute-start.21 = (bf16[4,96,384]{2,1,0:T(8,128)(2,1)}, bf16[4,96,384]{2,1,0:T(8,128)(2,1)}, u32[]{:S(2)}, u32[]{:S(2)}) collective-permute-start(bf16[4,96,384]{2,1,0:T(8,128)(2,1)} %collective-permute-done.20), channel_id=1, source_target_pairs={{0,4},{4,8},{8,12},{12,0},{1,5},{5,9},{9,13},{13,1},{2,6},{6,10},{... | collective-permute-start | bytes 884744 | tf_op jit(solution)/shard_map/ppermute | solution.py:162
  227.3 19.0 %collective-permute-start.17 = (bf16[384,384]{1,0:T(8,128)(2,1)}, bf16[384,384]{1,0:T(8,128)(2,1)}, u32[]{:S(2)}, u32[]{:S(2)}) collective-permute-start(bf16[384,384]{1,0:T(8,128)(2,1)} %collective-permute-done.15), channel_id=1, source_target_pairs={{0,4},{4,8},{8,12},{12,0},{1,5},{5,9},{9,13},{13,1},{2,6},{6,10},{... | collective-permute-start | bytes 884744 | tf_op jit(solution)/shard_map/ppermute | solution.py:162
  233.4 18.7 %collective-permute-start.18 = (bf16[384,384]{1,0:T(8,128)(2,1)}, bf16[384,384]{1,0:T(8,128)(2,1)}, u32[]{:S(2)}, u32[]{:S(2)}) collective-permute-start(bf16[384,384]{1,0:T(8,128)(2,1)} %collective-permute-done.16), channel_id=1, source_target_pairs={{0,12},{4,0},{8,4},{12,8},{1,13},{5,1},{9,5},{13,9},{2,14},{6,2},{... | collective-permute-start | bytes 884744 | tf_op jit(solution)/shard_map/ppermute | solution.py:162
  236.9 18.3 %collective-permute-start.1 = (bf16[512,512]{1,0:T(8,128)(2,1)S(1)}, bf16[512,512]{1,0:T(8,128)(2,1)S(1)}, u32[]{:S(2)}, u32[]{:S(2)}) collective-permute-start(bf16[512,512]{1,0:T(8,128)(2,1)S(1)} %add_convert_fusion), channel_id=1, source_target_pairs={{0,2},{2,0},{1,3},{3,1},{4,6},{6,4},{5,7},{7,5},{8,10},{10,8},{9,1... | collective-permute-start | bytes 1572872 | tf_op jit(solution)/shard_map/ppermute | solution.py:192
  (25 other events, 71.9 us)
Sparse Core Ops, SparseCore 0:
  11.7 22.3 all-gather.4
  48.5 18.7 all-gather.2
